TPU v7x, 32 devices: a whole 2x2x4 slice. The times are simulated.
32 devices in a mesh: expert: 4 (over y, x), context: 4 (over z), dp: 2 (over core).
Axes of the slice: x: 2, y: 2, z: 4, core: 2. Of those that a mesh axis runs over, the one named last changes fastest.
Arguments:
- layer_input: bfloat16 [8, 1024, 1536], P(('expert', 'dp'), 'context'), may hold values from -6 to 6
- cotangent: bfloat16 [8, 1024, 1536], P(('expert', 'dp'), 'context'), may hold values from -6 to 6
- block_order: int32 [8, 8], P(('expert', 'dp')), may hold values from 0 to 7, each once within a row
- routes: int32 [8, 1024, 8], P(('expert', 'dp'), 'context'), may hold values from 0 to 19, all different within a row; in each aligned block of 256 rows (0 to 255, 256 to 511, ..., all dimensions but the last counted through in order) at most 200 rows name the same one
- route_gates: float32 [8, 1024, 8], P(('expert', 'dp'), 'context'), may hold values from 0.06 to 0.25
- joined_weight: float32 [1536, 2560], P(('expert', 'context', 'dp')), may hold values from -0.15625 to 0.15625
- joined_first: float32 [1536, 2560], P(('expert', 'context', 'dp')), may hold values from -128 to 128
- joined_second: float32 [1536, 2560], P(('expert', 'context', 'dp')), may hold values from 1720.32 to 6881.28
- output_weight: float32 [1536, 1536], P(None, ('expert', 'context', 'dp')), may hold values from -1.25 to 1.25
- output_first: float32 [1536, 1536], P(None, ('expert', 'context', 'dp')), may hold values from -16 to 16
- output_second: float32 [1536, 1536], P(None, ('expert', 'context', 'dp')), may hold values from 38.5024 to 155.648
- norm_gains: float32 [2, 1536], P(None, ('expert', 'context', 'dp')), may hold values from 0.5 to 1.5
- gains_first: float32 [2, 1536], P(None, ('expert', 'context', 'dp')), may hold values from -128 to 128
- gains_second: float32 [2, 1536], P(None, ('expert', 'context', 'dp')), may hold values from 1720.32 to 6881.28
- expand_weight: float32 [20, 1536, 1024], P('expert', ('context', 'dp')), may hold values from -0.15625 to 0.15625
- expand_first: float32 [20, 1536, 1024], P('expert', ('context', 'dp')), may hold values from -28 to 28
- expand_second: float32 [20, 1536, 1024], P('expert', ('context', 'dp')), may hold values from 84.5208 to 337.428
- contract_weight: float32 [20, 512, 1536], P('expert', None, ('context', 'dp')), may hold values from -1 to 1
- contract_first: float32 [20, 512, 1536], P('expert', None, ('context', 'dp')), may hold values from -6 to 6
- contract_second: float32 [20, 512, 1536], P('expert', None, ('context', 'dp')), may hold values from 1.104012 to 4.4226
Outputs:
- output: bfloat16 [8, 1024, 1536], P(('expert', 'dp'), 'context')
- grad_input: bfloat16 [8, 1024, 1536], P(('expert', 'dp'), 'context')
- joined_new: float32 [1536, 2560], P(('expert', 'context', 'dp'))
- joined_first_new: float32 [1536, 2560], P(('expert', 'context', 'dp'))
- joined_second_new: float32 [1536, 2560], P(('expert', 'context', 'dp'))
- output_new: float32 [1536, 1536], P(None, ('expert', 'context', 'dp'))
- output_first_new: float32 [1536, 1536], P(None, ('expert', 'context', 'dp'))
- output_second_new: float32 [1536, 1536], P(None, ('expert', 'context', 'dp'))
- gains_new: float32 [2, 1536], P(None, ('expert', 'context', 'dp'))
- gains_first_new: float32 [2, 1536], P(None, ('expert', 'context', 'dp'))
- gains_second_new: float32 [2, 1536], P(None, ('expert', 'context', 'dp'))
- expand_new: float32 [20, 1536, 1024], P('expert', ('context', 'dp'))
- expand_first_new: float32 [20, 1536, 1024], P('expert', ('context', 'dp'))
- expand_second_new: float32 [20, 1536, 1024], P('expert', ('context', 'dp'))
- contract_new: float32 [20, 512, 1536], P('expert', None, ('context', 'dp'))
- contract_first_new: float32 [20, 512, 1536], P('expert', None, ('context', 'dp'))
- contract_second_new: float32 [20, 512, 1536], P('expert', None, ('context', 'dp'))
Inputs may be any that keep to these rules, and one draw needn't show every extreme that they name: `routes`: each row names 8 different experts. Within the rows of one device (aligned blocks of 256 tokens) no expert is named more than 200 times, and in every draw some expert is named exactly 200 times by the rows of some device. Each row is a permutation; stored block j of a sequence (its rows j * 128 to j * 128 + 127) holds positions block_order[s, j] * 128 onward in order.
All inputs are finite; a program needn't handle non-finite values.
Results may differ from a plain program's by a relative error of at most 0.024.
Values may be sent and summed in bfloat16 or wider, within the bound.
No kernel may reach another device: no remote copies, remote signals or barrier semaphores. Data moves between devices by JAX's collectives and lax.ppermute only.
A program may use at most 384 MiB of HBM per device.

v0:
```python
import functools
import math

import jax
import jax.numpy as jnp
import numpy as np
from jax import lax
from jax.experimental import pallas as pl
from jax.experimental.pallas import tpu as pltpu
from jax.sharding import PartitionSpec as P

HEADS = 24
KV_HEADS = 8
HEAD_DIM = 64
FF = 512
TOP = 8
STEP = 10
GROUPS = HEADS // KV_HEADS
PAIRS = KV_HEADS // 2
QUERY_WIDTH = HEADS * HEAD_DIM
KV_WIDTH = KV_HEADS * HEAD_DIM
PAIR_WIDTH = 2 * GROUPS * HEAD_DIM
LANES = 128
VMEM_BYTES = 60 * 1024 * 1024
TOKEN = (8, 128)
SCALAR = pl.BlockSpec(memory_space=pltpu.SMEM)

norm_eps = 1e-06
beta_one = 0.9
beta_two = 0.95
adam_eps = 1e-08
decay_rate = 0.1
rate_joined = 0.08
rate_output = 0.6
rate_gains = 0.6
rate_expand = 0.08
rate_contract = 0.5
masked_score = -1e30

low = jnp.bfloat16
wide = jnp.float32


def adamw(weight, first, second, grad, rate, decay):
    first_new = beta_one * first + (1.0 - beta_one) * grad
    second_new = beta_two * second + (1.0 - beta_two) * grad * grad
    first_hat = first_new / (1.0 - beta_one**STEP)
    second_hat = second_new / (1.0 - beta_two**STEP)
    weight_new = weight - rate * (first_hat / (jnp.sqrt(second_hat) + adam_eps) + decay * weight)
    return (weight_new, first_new, second_new)


def dot_nn(left, right):
    return lax.dot_general(left, right, (((1,), (0,)), ((), ())), preferred_element_type=wide)


def dot_nt(left, right):
    return lax.dot_general(left, right, (((1,), (1,)), ((), ())), preferred_element_type=wide)


def pair_order(groups):
    half = HEAD_DIM // 2
    old = np.arange(2 * groups * HEAD_DIM).reshape(2, groups, 2, half)
    return old.transpose(1, 2, 0, 3).reshape(-1)


def order_matrix(groups):
    order = pair_order(groups)
    size = order.shape[0]
    return jnp.asarray(np.arange(size)[:, None] == order[None, :], dtype=low)


def reorder_columns(rows, back=False):
    count = rows.shape[0]
    query_mat = order_matrix(GROUPS)
    key_mat = order_matrix(1)
    kv = rows[:, QUERY_WIDTH:]
    if back:
        query_mat = query_mat.T
        key_mat = key_mat.T
        kv = jnp.swapaxes(kv.reshape(count, PAIRS, 2, LANES), 1, 2)
    else:
        kv = jnp.swapaxes(kv.reshape(count, 2, PAIRS, LANES), 1, 2)
    exact = lax.Precision.HIGHEST if rows.dtype == wide else None
    query = jnp.einsum(
        "rpo,on->rpn",
        rows[:, :QUERY_WIDTH].reshape(count, PAIRS, PAIR_WIDTH),
        query_mat.astype(rows.dtype),
        precision=exact,
        preferred_element_type=wide,
    ).reshape(count, QUERY_WIDTH)
    others = jnp.einsum(
        "rpo,on->rpn",
        kv.reshape(count, 2 * PAIRS, LANES),
        key_mat.astype(rows.dtype),
        precision=exact,
        preferred_element_type=wide,
    ).reshape(count, 2 * KV_WIDTH)
    return jnp.concatenate([query, others], axis=1)


def swap(block, axis, step):
    count = lax.axis_size(axis)
    return lax.ppermute(block, axis, [(i, i ^ step) for i in range(count)])


def spread(block, axis):
    return [block] + [swap(block, axis, k) for k in range(1, lax.axis_size(axis))]


def after(value, *others):
    return lax.optimization_barrier((value, *others))[0]


def all_after(values, *others):
    count = len(values)
    return list(lax.optimization_barrier((*values, *others))[:count])


def share(block, axis):
    return trade(jnp.broadcast_to(block[None], (lax.axis_size(axis), *block.shape)), axis)


def trade(blocks, axis):
    return lax.all_to_all(blocks, axis, split_axis=0, concat_axis=0, tiled=True)


def in_order(parts, own):
    rows = parts[0].shape[0]
    joined = jnp.zeros((len(parts) * rows, *parts[0].shape[1:]), parts[0].dtype)
    for k, part in enumerate(parts):
        joined = lax.dynamic_update_slice_in_dim(joined, part, (own ^ k) * rows, 0)
    return joined


class OwnerSum:
    def __init__(self, own, other, shape):
        self.own = own.reshape(shape)
        self.came = swap(other, "dp", 1).reshape(shape)

    def spread_experts(self, *others):
        came = after(self.came, *others)
        both = [
            (self.own[k].astype(wide) + came[k].astype(wide)).astype(low)
            for k in range(self.own.shape[0])
        ]
        self.parts = [both[0]] + [swap(both[k], "expert", k) for k in range(1, len(both))]
        return both

    def spread_contexts(self, *others):
        parts = all_after(self.parts, *others)
        total = functools.reduce(jnp.add, [part.astype(wide) for part in parts])
        column = [total[k].astype(low) for k in range(1, total.shape[0])]
        self.parts = [total[0]] + [swap(part, "context", k + 1) for k, part in enumerate(column)]
        return column

    def finish(self, *others):
        parts = all_after(self.parts, *others)
        return functools.reduce(jnp.add, [part.astype(wide) for part in parts])


def call(body, grid, in_specs, out_specs, out_shape, scratch=(), aliases=None):
    order = pl.BlockSpec(TOKEN, lambda *_: (0, 0))

    def ordered(*refs):
        place = len(in_specs)
        body(*refs[:place], *refs[place + 1 :])

    return pl.pallas_call(
        ordered,
        grid=grid,
        in_specs=[*in_specs, order],
        out_specs=out_specs,
        out_shape=out_shape,
        scratch_shapes=list(scratch),
        input_output_aliases=aliases or {},
        compiler_params=pltpu.CompilerParams(vmem_limit_bytes=VMEM_BYTES),
        cost_estimate=pl.CostEstimate(flops=1, bytes_accessed=1, transcendentals=0),
    )


def token(*others):
    return lax.optimization_barrier((jnp.zeros(TOKEN, wide), *others))[0]


def turn(vals, cosine, sine):
    return vals * cosine + pltpu.roll(vals, LANES // 2, 1) * sine


def project_body(count, rows_ref, scale_ref, cos_ref, sin_ref, *refs):
    weight_refs, (query_ref, kv_ref, weight_ref) = refs[:count], refs[count:]
    step = pl.program_id(0)
    depth = weight_refs[0].shape[0]
    for k in range(count):
        weight_ref[k * depth : (k + 1) * depth, :] = weight_refs[k][...]
    total = dot_nn(rows_ref[...], weight_ref[...]) * scale_ref[...]
    block = total.shape[1]
    query_steps = QUERY_WIDTH // block
    cosine, sine = cos_ref[...], sin_ref[...]
    groups = [total[:, i * LANES : (i + 1) * LANES] for i in range(block // LANES)]

    @pl.when(step < query_steps)
    def _():
        for i, group in enumerate(groups):
            turned = turn(group, cosine, sine) * HEAD_DIM**-0.5
            query_ref[:, i * LANES : (i + 1) * LANES] = turned.astype(low)

    @pl.when(step >= query_steps)
    def _():
        for i, group in enumerate(groups):
            kept = turn(group, cosine, sine) if i % 2 == 0 else group
            kv_ref[:, i * LANES : (i + 1) * LANES] = kept.astype(low)


def project(rows, scale, cosine, sine, weights, order):
    tokens, width = rows.shape
    columns = QUERY_WIDTH + 2 * KV_WIDTH
    block = 512
    query_steps = QUERY_WIDTH // block
    depth = weights[0].shape[0]
    whole = lambda shape: pl.BlockSpec(shape, lambda j: (0, 0))
    return call(
        functools.partial(project_body, len(weights)),
        (columns // block,),
        [whole((tokens, width)), whole((tokens, 1)), whole((tokens, LANES)), whole((tokens, LANES))]
        + [pl.BlockSpec((depth, block), lambda j: (0, j))] * len(weights),
        [
            pl.BlockSpec((tokens, block), lambda j: (0, jnp.minimum(j, query_steps - 1))),
            pl.BlockSpec((tokens, block), lambda j: (0, jnp.maximum(j - query_steps, 0))),
        ],
        [
            jax.ShapeDtypeStruct((tokens, QUERY_WIDTH), low),
            jax.ShapeDtypeStruct((tokens, 2 * KV_WIDTH), low),
        ],
        scratch=[pltpu.VMEM((width, block), low)],
    )(rows, scale, cosine, sine, *weights, order)


def lane_of(shape, axis, which):
    place = lax.broadcasted_iota(jnp.int32, shape, axis)
    return ((place // (HEAD_DIM // 2)) % 2) == which


def stack_heads(block, which):
    keep = lane_of((block.shape[0], LANES), 1, which)
    return jnp.concatenate(
        [
            jnp.where(keep, block[:, g * LANES : (g + 1) * LANES], jnp.zeros((), block.dtype))
            for g in range(GROUPS)
        ],
        axis=0,
    )


def allowed_pairs(key_pos, query_pos):
    seen = key_pos <= query_pos
    return jnp.concatenate([seen] * GROUPS, axis=1)


def turned_block(block):
    return block.astype(wide).T.astype(low)


def attend_body(count, query_ref, key_pos_ref, query_pos_ref, *refs):
    kv_refs, (out_ref, out_low_ref, log_ref) = refs[:count], refs[count:]
    tokens = query_ref.shape[0]
    seen = allowed_pairs(key_pos_ref[...], query_pos_ref[...])
    keys = jnp.concatenate([ref[:, :LANES] for ref in kv_refs], axis=0)
    values = jnp.concatenate([turned_block(ref[:, LANES:]) for ref in kv_refs], axis=1)
    outs = []
    for which in range(2):
        query = stack_heads(query_ref[...], which)
        scores = jnp.where(seen, dot_nt(keys, query), masked_score)
        peak = jnp.max(scores, axis=0, keepdims=True)
        weight = jnp.exp(scores - peak)
        total = jnp.sum(weight, axis=0, keepdims=True)
        outs.append(dot_nn(values, weight.astype(low)) / total)
        log_ref[0, which : which + 1, :] = peak + jnp.log(total)
    first = lane_of(outs[0].shape, 0, 0)
    both = jnp.where(first, outs[0], outs[1]).T
    for g in range(GROUPS):
        piece = both[g * tokens : (g + 1) * tokens, :]
        out_ref[:, g * LANES : (g + 1) * LANES] = piece
        out_low_ref[:, g * LANES : (g + 1) * LANES] = piece.astype(low)


def attend(query, key_pos, query_pos, kv_parts, order):
    tokens = query.shape[0]
    count = len(kv_parts)
    seq_len = tokens * count
    pairs = pl.BlockSpec((tokens, PAIR_WIDTH), lambda p: (0, p))
    return call(
        functools.partial(attend_body, count),
        (PAIRS,),
        [
            pairs,
            pl.BlockSpec((seq_len, 1), lambda p: (0, 0)),
            pl.BlockSpec((1, tokens), lambda p: (0, 0)),
        ]
        + [pl.BlockSpec((tokens, 2 * LANES), lambda p: (0, p))] * count,
        [pairs, pairs, pl.BlockSpec((1, 2, GROUPS * tokens), lambda p: (p, 0, 0))],
        [
            jax.ShapeDtypeStruct((tokens, QUERY_WIDTH), wide),
            jax.ShapeDtypeStruct((tokens, QUERY_WIDTH), low),
            jax.ShapeDtypeStruct((PAIRS, 2, GROUPS * tokens), wide),
        ],
    )(query, key_pos, query_pos, *kv_parts, order)


def attend_back_body(count, own_ref, query_ref, grad_ref, out_ref, log_ref, key_pos_ref, query_pos_ref,
                     scale_ref, cos_ref, sin_ref, *refs):
    kv_refs, (grad_query_ref, grad_kv_ref) = refs[:count], refs[count:]
    tokens = query_ref.shape[0]
    grads = grad_ref[...]
    product = jnp.concatenate(
        [
            (grads[:, g * LANES : (g + 1) * LANES].astype(wide)
             * out_ref[:, g * LANES : (g + 1) * LANES]).T
            for g in range(GROUPS)
        ],
        axis=1,
    )
    first = lane_of(product.shape, 0, 0)
    delta = [
        jnp.sum(jnp.where(first, product, 0.0), axis=0, keepdims=True),
        jnp.sum(jnp.where(first, 0.0, product), axis=0, keepdims=True),
    ]
    seen = allowed_pairs(key_pos_ref[...], query_pos_ref[...])
    keys = jnp.concatenate([ref[:, :LANES] for ref in kv_refs], axis=0)
    values = jnp.concatenate([ref[:, LANES:] for ref in kv_refs], axis=0)
    keys_turned = jnp.concatenate([turned_block(ref[:, :LANES]) for ref in kv_refs], axis=1)
    grad_key, grad_value, grad_query = None, None, []
    for which in range(2):
        query = stack_heads(query_ref[...], which)
        head = stack_heads(grads, which)
        scores = jnp.where(seen, dot_nt(keys, query), masked_score)
        probs = jnp.exp(scores - log_ref[0, which : which + 1, :])
        grad_probs = dot_nt(values, head)
        grad_scores = (probs * (grad_probs - delta[which])).astype(low)
        part_value = dot_nn(probs.astype(low), head)
        part_key = dot_nn(grad_scores, query)
        grad_query.append(dot_nn(keys_turned, grad_scores))
        grad_value = part_value if grad_value is None else grad_value + part_value
        grad_key = part_key if grad_key is None else grad_key + part_key
    scale, cosine, sine = scale_ref[...], cos_ref[...], sin_ref[...]
    for k in range(count):
        rows = slice(k * tokens, (k + 1) * tokens)
        grad_kv_ref[own_ref[0] ^ k, :, :LANES] = grad_key[rows, :].astype(low)
        grad_kv_ref[own_ref[0] ^ k, :, LANES:] = grad_value[rows, :].astype(low)
    first = lane_of(grad_query[0].shape, 0, 0)
    both = (jnp.where(first, grad_query[0], grad_query[1]) * HEAD_DIM**-0.5).T
    for g in range(GROUPS):
        piece = both[g * tokens : (g + 1) * tokens, :]
        back = turn(piece, cosine, -sine) * scale
        grad_query_ref[:, g * LANES : (g + 1) * LANES] = back.astype(low)


def attend_back(
    own, query, grads, out, logs, key_pos, query_pos, scale, cosine, sine, kv_parts, order
):
    tokens = query.shape[0]
    count = len(kv_parts)
    seq_len = tokens * count
    pairs = pl.BlockSpec((tokens, PAIR_WIDTH), lambda p: (0, p))
    whole = lambda shape: pl.BlockSpec(shape, lambda p: (0, 0))
    part = pl.BlockSpec((tokens, 2 * LANES), lambda p: (0, p))
    return call(
        functools.partial(attend_back_body, count),
        (PAIRS,),
        [
            SCALAR,
            pairs,
            pairs,
            pairs,
            pl.BlockSpec((1, 2, GROUPS * tokens), lambda p: (p, 0, 0)),
            whole((seq_len, 1)),
            whole((1, tokens)),
            whole((tokens, 1)),
            whole((tokens, LANES)),
            whole((tokens, LANES)),
        ]
        + [part] * count,
        [pairs, pl.BlockSpec((count, tokens, 2 * LANES), lambda p: (0, 0, p))],
        [
            jax.ShapeDtypeStruct((tokens, QUERY_WIDTH), low),
            jax.ShapeDtypeStruct((count, tokens, 2 * KV_WIDTH), low),
        ],
    )(own, query, grads, out, logs, key_pos, query_pos, scale, cosine, sine, *kv_parts, order)


def hidden_body(count, first, own_ref, grads_ref, gate_ref, weight_ref, *refs):
    part_refs, (hidden_ref, back_ref, rows_ref) = refs[:count], refs[count:]
    expert, place = pl.program_id(0), pl.program_id(1)
    block = grads_ref.shape[0]
    tokens = part_refs[0].shape[0]

    @pl.when((expert == 0) & (place == 0))
    def _():
        for k, part_ref in enumerate(part_refs):
            start = pl.multiple_of((own_ref[0] ^ k) * tokens, tokens)
            rows_ref[pl.ds(start, tokens), :] = part_ref[...]

    rows = rows_ref[pl.ds(pl.multiple_of(place * block, block), block), :]
    grads = grads_ref[...]
    lane = lax.broadcasted_iota(jnp.int32, gate_ref.shape, 1)
    weight = jnp.sum(
        jnp.where(lane == expert + first, gate_ref[...], 0.0), axis=1, keepdims=True
    )
    step = 256
    for h in range(0, FF, step):
        gate = dot_nn(rows, weight_ref[0, :, h : h + step])
        up = dot_nn(rows, weight_ref[0, :, FF + h : FF + h + step])
        grad_hidden = dot_nn(grads, weight_ref[0, :, 2 * FF + h : 2 * FF + h + step]) * weight
        sigmoid = 1.0 / (1.0 + jnp.exp(-gate))
        active = gate * sigmoid
        hidden_ref[0, :, h : h + step] = (active * up * weight).astype(low)
        slope = sigmoid + active * (1.0 - sigmoid)
        back_ref[0, :, h : h + step] = (grad_hidden * up * slope).astype(low)
        back_ref[0, :, FF + h : FF + h + step] = (grad_hidden * active).astype(low)


def expert_hidden(own, parts, grads, gates, first, weights, order):
    tokens, width = grads.shape
    experts = weights.shape[0]
    block = min(tokens, 1024)
    part_rows = parts[0].shape[0]
    return call(
        functools.partial(hidden_body, len(parts), first),
        (experts, tokens // block),
        [
            SCALAR,
            pl.BlockSpec((block, width), lambda e, t: (t, 0)),
            pl.BlockSpec((block, gates.shape[1]), lambda e, t: (t, 0)),
            pl.BlockSpec((1, width, 3 * FF), lambda e, t: (e, 0, 0)),
        ]
        + [
            pl.BlockSpec((part_rows, width), lambda e, t: (0, 0), pipeline_mode=pl.Buffered(1))
        ]
        * len(parts),
        [
            pl.BlockSpec((1, block, FF), lambda e, t: (e, t, 0)),
            pl.BlockSpec((1, block, 2 * FF), lambda e, t: (e, t, 0)),
        ],
        [
            jax.ShapeDtypeStruct((experts, tokens, FF), low),
            jax.ShapeDtypeStruct((experts, tokens, 2 * FF), low),
        ],
        scratch=[pltpu.VMEM((tokens, width), low)],
    )(own, grads, gates, weights, *parts, order)


def turn_body(count, own_ref, *refs):
    part_refs, out_ref = refs[:count], refs[count]
    tokens = part_refs[0].shape[0]
    for k, part_ref in enumerate(part_refs):
        start = pl.multiple_of((own_ref[0] ^ k) * tokens, tokens)
        out_ref[:, pl.ds(start, tokens)] = turned_block(part_ref[...])


def turn_rows(own, parts, order):
    count = len(parts)
    if count == 1:
        count = parts[0].shape[0] // 256
    width = parts[0].shape[1]
    tokens = parts[0].shape[0] if len(parts) > 1 else 256
    specs = [
        pl.BlockSpec((tokens, width), (lambda i, k=k: (k, 0)) if len(parts) == 1 else (lambda i: (0, 0)))
        for k in range(count)
    ]
    return call(
        functools.partial(turn_body, count),
        (1,),
        [SCALAR, *specs],
        pl.BlockSpec((width, count * tokens), lambda i: (0, 0)),
        jax.ShapeDtypeStruct((width, count * tokens), low),
    )(own, *(parts * count if len(parts) == 1 else parts), order)


def weight_grad_body(sizes, rows_ref, grads_ref, *refs):
    count = len(sizes)
    back_refs, hidden_refs, out_ref = refs[:count], refs[count : 2 * count], refs[2 * count]
    step = pl.program_id(0)
    start = 0
    for back_ref, hidden_ref, size in zip(back_refs, hidden_refs, sizes):

        @pl.when((step >= start) & (step < start + size))
        def _():
            out_ref[0, :, : 2 * FF] = dot_nn(rows_ref[...], back_ref[0]).astype(low)
            out_ref[0, :, 2 * FF :] = dot_nn(grads_ref[...], hidden_ref[0]).astype(low)

        start += size


def expert_weight_grads(rows_turned, grads_turned, parts, order):
    width, tokens = rows_turned.shape
    sizes = [last - first for _, _, first, last in parts]
    firsts = [first for _, _, first, _ in parts]
    starts = [sum(sizes[:i]) for i in range(len(sizes))]
    block = width // 2
    place = lambda e, first, start, size: first + jnp.clip(e - start, 0, size - 1)

    def specs(depth):
        return [
            pl.BlockSpec((1, tokens, depth), lambda e, m, f=f, s=s, n=n: (place(e, f, s, n), 0, 0))
            for f, s, n in zip(firsts, starts, sizes)
        ]

    return call(
        functools.partial(weight_grad_body, sizes),
        (sum(sizes), width // block),
        [
            pl.BlockSpec((block, tokens), lambda e, m: (m, 0)),
            pl.BlockSpec((block, tokens), lambda e, m: (m, 0)),
            *specs(2 * FF),
            *specs(FF),
        ],
        pl.BlockSpec((1, block, 3 * FF), lambda e, m: (e, m, 0)),
        jax.ShapeDtypeStruct((sum(sizes), width, 3 * FF), low),
    )(
        rows_turned,
        grads_turned,
        *[back for _, back, _, _ in parts],
        *[hidden for hidden, _, _, _ in parts],
        order,
    )


def combine_body(sizes, own_ref, *refs):
    count = len(sizes)
    part_refs, weight_refs = refs[:count], refs[count : 2 * count]
    out_refs, total_ref = refs[2 * count : -1], refs[-1]
    step = pl.program_id(0)

    @pl.when(step == 0)
    def _():
        total_ref[...] = jnp.zeros_like(total_ref)

    start = 0
    for part_ref, weight_ref, size in zip(part_refs, weight_refs, sizes):

        @pl.when((step >= start) & (step < start + size))
        def _():
            total_ref[...] += dot_nt(part_ref[0], weight_ref[0])

        start += size

    @pl.when(step == start - 1)
    def _():
        tokens = out_refs[0].shape[0]
        for k, out_ref in enumerate(out_refs):
            place = pl.multiple_of((own_ref[0] ^ k) * tokens, tokens)
            out_ref[...] = total_ref[pl.ds(place, tokens), :].astype(low)


def combine(own, owners, parts, weights, column, order):
    tokens, depth = parts[0].shape[1:]
    width = weights[0].shape[1]
    sizes = [w.shape[0] for w in weights]
    starts = [sum(sizes[:i]) for i in range(len(sizes))]
    place = lambda e, start, size: jnp.clip(e - start, 0, size - 1)
    part_specs = [
        pl.BlockSpec((1, tokens, depth), lambda e, s=s, n=n: (place(e, s, n), 0, 0))
        for s, n in zip(starts, sizes)
    ]
    weight_specs = [
        pl.BlockSpec((1, width, depth), lambda e, s=s, n=n: (place(e, s, n), 0, column))
        for s, n in zip(starts, sizes)
    ]
    return call(
        functools.partial(combine_body, sizes),
        (sum(sizes),),
        [SCALAR] + part_specs + weight_specs,
        [pl.BlockSpec((tokens // owners, width), lambda e: (0, 0))] * owners,
        [jax.ShapeDtypeStruct((tokens // owners, width), low)] * owners,
        scratch=[pltpu.VMEM((tokens, width), wide)],
    )(own, *parts, *weights, order)


def norm_back_body(count, scale_ref, gain_ref, middle_ref, cotangent_ref, weight_ref, *refs):
    part_refs = refs[:count]
    middle_grad_ref, turned_ref, attended_ref, gain_grad_ref, proj_ref = refs[count:]

    @pl.when(pl.program_id(0) == 0)
    def _():
        grad = functools.reduce(jnp.add, [ref[...].astype(wide) for ref in part_refs])
        scale = scale_ref[...]
        unit = middle_ref[...] * scale
        gain_grad_ref[...] = jnp.sum(grad * unit, axis=0, keepdims=True)
        grad = grad * gain_ref[...]
        mean = jnp.mean(grad * unit, axis=1, keepdims=True)
        grad = cotangent_ref[...].astype(wide) + scale * (grad - unit * mean)
        middle_grad_ref[...] = grad
        proj_ref[...] = grad.astype(low)
        turned_ref[...] = grad.T.astype(low)

    attended_ref[...] = dot_nn(proj_ref[...], weight_ref[...]).astype(low)


def norm_back_two(parts, middle, scale, gain, cotangent, output_pack, order):
    tokens, width = middle.shape
    block = 512
    whole = lambda shape: pl.BlockSpec(shape, lambda j: (0, 0))
    return call(
        functools.partial(norm_back_body, len(parts)),
        (QUERY_WIDTH // block,),
        [
            whole((tokens, 1)),
            whole((1, width)),
            whole((tokens, width)),
            whole((tokens, width)),
            pl.BlockSpec((width, block), lambda j: (0, j)),
        ]
        + [whole((tokens, width))] * len(parts),
        [
            whole((tokens, width)),
            whole((width, tokens)),
            pl.BlockSpec((tokens, block), lambda j: (0, j)),
            whole((1, width)),
        ],
        [
            jax.ShapeDtypeStruct((tokens, width), wide),
            jax.ShapeDtypeStruct((width, tokens), low),
            jax.ShapeDtypeStruct((tokens, QUERY_WIDTH), low),
            jax.ShapeDtypeStruct((1, width), wide),
        ],
        scratch=[pltpu.VMEM((tokens, width), low)],
    )(scale, gain, middle, cotangent, output_pack, *parts, order)


def outer_body(input_ref, proj_ref, gain_ref, query_ref, attended_ref, out_ref):
    out_ref[:, :QUERY_WIDTH] = dot_nn(input_ref[...], query_ref[...]).astype(low)
    out_ref[:, QUERY_WIDTH : 2 * QUERY_WIDTH] = dot_nn(proj_ref[...], attended_ref[...]).astype(low)
    out_ref[:, 2 * QUERY_WIDTH :] = jnp.broadcast_to(
        gain_ref[...], (gain_ref.shape[0], LANES)
    ).astype(low)


def outer_grads(half, cores, input_turned, proj_turned, gain_grads, grad_query, attended, order):
    width, tokens = input_turned.shape
    rows = width // cores
    part = lambda columns: pl.BlockSpec((rows, columns), lambda i: (half, 0))
    whole = pl.BlockSpec((tokens, QUERY_WIDTH), lambda i: (0, 0))
    columns = 2 * QUERY_WIDTH + LANES
    return call(
        outer_body,
        (1,),
        [part(tokens), part(tokens), part(1), whole, whole],
        pl.BlockSpec((rows, columns), lambda i: (0, 0)),
        jax.ShapeDtypeStruct((rows, columns), low),
    )(input_turned, proj_turned, gain_grads, grad_query, attended, order)


def kv_body(parts_ref, scale_ref, cos_ref, sin_ref, input_ref, grad_ref, *out_refs):
    total = jnp.sum(parts_ref[...].astype(wide), axis=0)
    cosine, sine, scale = cos_ref[...], sin_ref[...], scale_ref[...]
    for i in range(2 * PAIRS):
        group = total[:, i * LANES : (i + 1) * LANES]
        group = turn(group, cosine, -sine) if i % 2 == 0 else group
        grad_ref[:, i * LANES : (i + 1) * LANES] = (group * scale).astype(low)
    grads = grad_ref[...]
    rows = out_refs[0].shape[0]
    for k, out_ref in enumerate(out_refs):
        out_ref[...] = dot_nn(input_ref[k * rows : (k + 1) * rows, :], grads).astype(low)


def kv_grads(cores, parts, scale, cosine, sine, input_turned, order):
    tokens, columns = parts.shape[1:]
    width = input_turned.shape[0]
    shapes = [(tokens, columns)] + [(width // cores, columns)] * cores
    whole = lambda shape: pl.BlockSpec(shape, lambda i: (0,) * len(shape))
    return call(
        kv_body,
        (1,),
        [
            whole(parts.shape),
            whole((tokens, 1)),
            whole((tokens, LANES)),
            whole((tokens, LANES)),
            whole((width, tokens)),
        ],
        [whole(shape) for shape in shapes],
        [jax.ShapeDtypeStruct(shape, low) for shape in shapes],
    )(parts, scale, cosine, sine, input_turned, order)


def input_body(count, rows, place_ref, query_ref, kv_ref, scale_ref, input_ref, middle_ref, *refs):
    weight_refs, (out_ref, turned_ref) = refs[:count], refs[count:]
    weights = jnp.concatenate([ref[...] for ref in weight_refs], axis=0)
    part = dot_nt(weights[:, :QUERY_WIDTH], query_ref[...])
    part += dot_nt(weights[:, QUERY_WIDTH:], kv_ref[...])
    for i in range(part.shape[0] // rows):
        start = pl.multiple_of(place_ref[i] * rows, rows)
        turned_ref[pl.ds(start, rows), :] = part[i * rows : (i + 1) * rows, :]
    grad = turned_ref[...].T
    unit = input_ref[...].astype(wide) * scale_ref[...]
    mean = jnp.mean(grad * unit, axis=1, keepdims=True)
    out_ref[...] = (middle_ref[...] + grad - unit * mean).astype(low)


def input_grads(place, grad_query, grad_kv, scale, rows, grad_middle, weights, order):
    tokens, width = rows.shape
    whole = lambda array: pl.BlockSpec(array.shape, lambda i: (0, 0))
    operands = [grad_query, grad_kv, scale, rows, grad_middle, *weights]
    return call(
        functools.partial(input_body, len(weights), width // place.shape[0]),
        (1,),
        [SCALAR] + [whole(operand) for operand in operands],
        pl.BlockSpec((tokens, width), lambda i: (0, 0)),
        jax.ShapeDtypeStruct((tokens, width), low),
        scratch=[pltpu.VMEM((width, tokens), wide)],
    )(place, *operands, order)


def adam_body(held, grad_ref, *refs):
    expand, contract, refs = refs[:3], refs[3:6], refs[6 + held :]
    grads = grad_ref[0].astype(wide)
    split = expand[0].shape[2]
    for arrays, grad, rate, out_refs in (
        (expand, grads[:, :split], rate_expand, refs[:3]),
        (contract, grads[:, split:].T, rate_contract, refs[3:]),
    ):
        results = adamw(*[array[0] for array in arrays], grad, rate, decay_rate)
        for out_ref, result in zip(out_refs, results):
            out_ref[0] = result


def adam_experts(first, grads, arrays, held, order):
    count = grads.shape[0]
    held = held or []
    block = lambda array: pl.BlockSpec((1, *array.shape[1:]), lambda e: (first + e, 0, 0))
    return call(
        functools.partial(adam_body, len(held)),
        (count,),
        [pl.BlockSpec((1, *grads.shape[1:]), lambda e: (e, 0, 0))]
        + [block(array) for array in arrays]
        + [pl.BlockSpec(memory_space=pl.ANY)] * len(held),
        [block(array) for array in arrays],
        [jax.ShapeDtypeStruct(array.shape, wide) for array in arrays],
        aliases={1 + len(arrays) + i: i for i in range(len(held))},
    )(grads, *arrays, *held, order)


def body(
    layer_input,
    cotangent,
    block_order,
    routes,
    route_gates,
    joined_weight,
    joined_first,
    joined_second,
    output_weight,
    output_first,
    output_second,
    norm_gains,
    gains_first,
    gains_second,
    expand_weight,
    expand_first,
    expand_second,
    contract_weight,
    contract_first,
    contract_second,
):
    experts_dev = expand_weight.shape[0]
    owners = lax.axis_size("expert")
    contexts = lax.axis_size("context")
    cores = lax.axis_size("dp")
    experts = experts_dev * owners
    tokens = layer_input.shape[1]
    width = layer_input.shape[2]
    half_block = tokens // 2
    slice_rows = joined_weight.shape[0]
    own_expert = lax.axis_index("expert")
    own_context = lax.axis_index("context")
    own_core = lax.axis_index("dp")

    gain_rows = norm_gains.astype(low).astype(wide).T
    joined_low = joined_weight.astype(low)
    joined_shard = reorder_columns((gain_rows[:, :1] * joined_low.astype(wide)).astype(low)).astype(low)
    query_mat = order_matrix(GROUPS)
    output_shard = jnp.einsum(
        "pod,on->dpn",
        output_weight.astype(low).reshape(PAIRS, PAIR_WIDTH, slice_rows),
        query_mat,
        preferred_element_type=wide,
    ).reshape(slice_rows, QUERY_WIDTH).astype(low)
    gain_column = jnp.broadcast_to(gain_rows[:, 1:].astype(low), (slice_rows, LANES))
    columns = joined_shard.shape[1]
    shard = jnp.concatenate([joined_shard, output_shard, gain_column], axis=1)

    bounds = [0, experts_dev // 2, experts_dev]
    chunks = list(zip(bounds[:-1], bounds[1:]))
    expert_low = [
        jnp.concatenate(
            [
                expand_weight[a:b].astype(low),
                jnp.swapaxes(contract_weight[a:b].astype(low), 1, 2),
            ],
            axis=2,
        )
        for a, b in chunks
    ]
    line, *expert_low = lax.optimization_barrier(
        (jnp.concatenate(spread(shard, "context"), axis=0), *expert_low)
    )
    joined_mine = spread(line[:, :columns], "expert")
    joined_parts = joined_mine + [swap(part, "dp", 1) for part in joined_mine]
    output_mine = share(after(line[:, columns:], *joined_mine), "expert")
    gather_expert = lambda part: lax.all_gather(part, ("context", "dp"), axis=1, tiled=True)
    expert_full = [gather_expert(expert_low[0])]

    ar = lambda n: jnp.arange(n, dtype=jnp.int32)
    to_relative = (
        ((own_expert ^ ar(owners))[None, :, None] * contexts + (own_context ^ ar(contexts))[None, None, :])
        * cores
        + (own_core ^ ar(cores))[:, None, None]
    ).reshape(-1)
    to_absolute = (
        (own_core ^ ar(cores))[None, None, :] * owners + (own_expert ^ ar(owners))[:, None, None]
    ) * contexts + (own_context ^ ar(contexts))[None, :, None]
    to_absolute = to_absolute.reshape(-1)
    slices = owners * contexts * cores

    def pick_rows(rows, index):
        return jnp.take(
            rows.reshape(slices, slice_rows, -1), index, axis=0, mode="clip", unique_indices=True
        ).reshape(rows.shape)

    hits = routes[0][:, :, None] == ar(experts)[None, None, :]
    gate_table = jnp.sum(jnp.where(hits, route_gates[0][:, :, None], 0.0), axis=1)
    gate_table = gate_table.reshape(tokens, owners, experts_dev)
    gate_sent = [
        lax.dynamic_index_in_dim(gate_table, own_expert ^ k, axis=1, keepdims=False)
        for k in range(owners)
    ]
    gate_parts = [gate_sent[0]] + [swap(gate_sent[k], "expert", k) for k in range(1, owners)]
    gates = in_order(gate_parts, own_expert)
    own = own_expert.reshape(1)
    zero = jnp.zeros((1,), jnp.int32)

    order = block_order[0]
    offsets = ar(half_block)

    def places_of(index):
        mine = lax.dynamic_slice_in_dim(order, 2 * index, 2)
        return (mine[:, None] * half_block + offsets[None, :]).reshape(-1)

    query_pos = places_of(own_context)
    key_pos = jnp.concatenate([places_of(own_context ^ k) for k in range(contexts)])
    half = HEAD_DIM // 2
    freq = jnp.exp(ar(half).astype(wide) * (2.0 / HEAD_DIM) * -math.log(10000.0))
    angle = query_pos.astype(wide)[:, None] * freq[None, :]
    cosine = jnp.tile(jnp.cos(angle), (1, 4))
    sine = jnp.sin(angle)
    sine = jnp.concatenate([-sine, -sine, sine, sine], axis=1)

    low_input = layer_input[0]
    resid = low_input.astype(wide)
    scale_one = lax.rsqrt(jnp.mean(resid * resid, axis=-1, keepdims=True) + norm_eps)
    unit_one = resid * scale_one
    input_turned = pick_rows(low_input.T, to_relative)
    input_relative = input_turned.T
    query, kv = project(input_relative, scale_one, cosine, sine, joined_parts, token())
    kv_parts = spread(kv, "context")
    output_mine = after(output_mine, kv)
    output_parts = [output_mine, swap(output_mine, "dp", 1)]
    out_grads = share(after(cotangent[0], output_mine), "expert").reshape(-1, width)
    output_place = (
        (own_core ^ ar(cores))[None, None, :] * owners + ar(owners)[:, None, None]
    ) * contexts + (own_context ^ ar(contexts))[None, :, None]
    output_pack = pick_rows(
        jnp.concatenate([part.reshape(-1, output_mine.shape[-1]) for part in output_parts], axis=0),
        output_place.reshape(-1),
    )
    output_turned = output_pack[:, :QUERY_WIDTH]
    gain_two = output_pack[:, QUERY_WIDTH].astype(wide)[None, :]
    kv_parts = all_after(kv_parts, output_pack)
    kv_parts, later = lax.optimization_barrier((kv_parts, expert_low[1:]))
    expert_full += [gather_expert(part) for part in later]
    attended_wide, attended, logs = attend(
        query, key_pos[:, None], query_pos[None, :], kv_parts, token()
    )
    middle = resid + dot_nt(attended, output_turned)
    scale_two = lax.rsqrt(jnp.mean(middle * middle, axis=-1, keepdims=True) + norm_eps)
    unit_two = middle * scale_two
    normed_two = (unit_two * gain_two).astype(low)

    row_parts = spread(normed_two, "expert")
    out_grads_turned = turn_rows(zero, [out_grads], token(normed_two))

    def grads_of(hidden, back, *others):
        return expert_weight_grads(
            rows_turned, out_grads_turned, [(hidden, back, 0, back.shape[0])], token(*others)
        )

    def to_owners(grads):
        return lax.psum_scatter(grads, ("context", "dp"), scatter_dimension=1, tiled=True)

    def to_tokens(parts):
        return [parts[0]] + [swap(parts[k], "expert", k) for k in range(1, owners)]

    cut = bounds[1]
    first_unit = expert_hidden(
        own, row_parts, out_grads, gates, 0, expert_full[0], token(out_grads_turned)
    )
    rows_turned = turn_rows(own, row_parts, token(first_unit[0]))
    first_grads = grads_of(*first_unit)
    second_unit = expert_hidden(
        own, row_parts, out_grads, gates, cut, expert_full[1], token(first_grads)
    )
    backs = [first_unit[1], second_unit[1]]
    grad_sent = combine(own, owners, backs, expert_full, 0, token())
    first_sum = to_owners(first_grads)
    grad_parts = to_tokens(grad_sent)
    second_grads = grads_of(*second_unit, *grad_sent)
    mixture_sent = combine(
        own, owners, [first_unit[0], second_unit[0]], expert_full, 2, token(second_grads)
    )
    mixture_parts = to_tokens(mixture_sent)

    grad_middle, proj_turned, grad_attended, gain_grad_two = norm_back_two(
        grad_parts, middle, scale_two, gain_two, cotangent[0], output_pack, token(*mixture_sent)
    )
    grad_query, grad_kv = attend_back(
        own_context.reshape(1), query, grad_attended, attended_wide, logs, key_pos[:, None], query_pos[None, :],
        scale_one, cosine, sine, kv_parts, token(grad_attended, first_sum),
    )
    expert_grads = [first_sum, to_owners(after(second_grads, first_sum))]
    grad_kv_parts = trade(grad_kv, "context")

    mixture = functools.reduce(
        jnp.add, [part.astype(wide) for part in all_after(mixture_parts, grad_query)]
    )
    output = (middle + mixture).astype(low)
    relative = (owners, contexts, slice_rows, -1)
    proj_turned = pick_rows(after(proj_turned, output), to_relative)
    gain_grads = pick_rows(gain_grad_two.reshape(width, 1), to_relative)
    other, own_part = [
        outer_grads(
            half, cores, input_turned, proj_turned, gain_grads, grad_query, attended, token()
        )
        for half in (1, 0)
    ]
    query_sum = OwnerSum(own_part, other, relative)
    latest = query_sum.spread_experts(own_part)
    latest = query_sum.spread_contexts(*latest)
    own_grad_kv, *kv_parts_sent = kv_grads(
        cores, grad_kv_parts, scale_one, cosine, sine, input_turned, token(*latest)
    )
    kv_sum = OwnerSum(*kv_parts_sent, relative)
    latest = kv_sum.spread_experts(own_grad_kv)
    if slice_rows % 16 == 0:
        grad_input = input_grads(
            to_relative, grad_query, own_grad_kv, scale_one, low_input, grad_middle, joined_parts,
            token(*latest),
        )
    else:
        grad_joined = jnp.concatenate([grad_query, own_grad_kv], axis=1)
        scaled_grad = jnp.concatenate([dot_nt(part, grad_joined) for part in joined_parts], axis=0)
        scaled_grad = pick_rows(scaled_grad, to_absolute).T
        grad_input = (
            grad_middle
            + scaled_grad
            - unit_one * jnp.mean(scaled_grad * unit_one, axis=-1, keepdims=True)
        ).astype(low)

    latest = kv_sum.spread_contexts(grad_input)
    arrays = [
        expand_weight, expand_first, expand_second, contract_weight, contract_first, contract_second
    ]
    expert_new = adam_experts(0, expert_grads[0], arrays, None, token(*latest))
    expert_new = adam_experts(cut, expert_grads[1], arrays, expert_new, token())
    expand_new, contract_new = expert_new[:3], expert_new[3:]
    sum_query = query_sum.finish(*latest, expand_new[0])
    sum_kv = kv_sum.finish(sum_query)
    sum_output = sum_query[:, QUERY_WIDTH:]
    sum_joined = jnp.concatenate([sum_query[:, :QUERY_WIDTH], sum_kv], axis=1)

    unit_grads = reorder_columns(sum_joined, back=True)
    sum_joined = gain_rows[:, :1] * unit_grads
    sum_gain_one = jnp.sum(joined_low.astype(wide) * unit_grads, axis=1)
    sum_gains = jnp.stack([sum_gain_one, sum_output[:, QUERY_WIDTH]], axis=0)
    sum_output_weight = jnp.einsum(
        "on,dpn->pod",
        query_mat.astype(wide),
        sum_output[:, :QUERY_WIDTH].reshape(slice_rows, PAIRS, PAIR_WIDTH),
        precision=lax.Precision.HIGHEST,
        preferred_element_type=wide,
    ).reshape(QUERY_WIDTH, slice_rows)
    joined_new = adamw(
        joined_weight, joined_first, joined_second, sum_joined, rate_joined, decay_rate
    )
    output_new = adamw(
        output_weight, output_first, output_second, sum_output_weight, rate_output, decay_rate
    )
    gains_new = adamw(norm_gains, gains_first, gains_second, sum_gains, rate_gains, 0.0)
    return (
        output.reshape(1, tokens, width),
        grad_input.reshape(1, tokens, width),
        *joined_new,
        *output_new,
        *gains_new,
        *expand_new,
        *contract_new,
    )


def solution(mesh):
    rows = P(("expert", "dp"), "context", None)
    joined = P(("expert", "context", "dp"), None)
    column = P(None, ("expert", "context", "dp"))
    expand = P("expert", ("context", "dp"), None)
    contract = P("expert", None, ("context", "dp"))
    placed = (
        (rows, rows, P(("expert", "dp"), None), rows, rows)
        + (joined,) * 3
        + (column,) * 6
        + (expand,) * 3
        + (contract,) * 3
    )
    return jax.shard_map(
        body,
        mesh=mesh,
        in_specs=placed,
        out_specs=(rows, rows) + placed[5:],
        check_vma=False,
    )
```

profile of v0, /device:TPU:9, one launch (start us, length us, event | category | flops | bytes accessed | tf_op | source)
XLA Modules:
  0.0 684.4 jit_solution(13564526293964678690)
XLA Ops:
  19.7 21.5 %collective-permute-done.2 = bf16[48,4224]{1,0:T(8,128)(2,1)} collective-permute-done((bf16[48,4224]{1,0:T(8,128)(2,1)}, bf16[48,4224]{1,0:T(8,128)(2,1)}, u32[]{:S(2)}, u32[]{:S(2)}) %collective-permute-start.2) | collective-permute-done | bytes 405536 | tf_op jit(solution)/shard_map/ppermute | solution.py:104
  41.2 7.6 %collective-permute-done.1 = bf16[48,4224]{1,0:T(8,128)(2,1)} collective-permute-done((bf16[48,4224]{1,0:T(8,128)(2,1)}, bf16[48,4224]{1,0:T(8,128)(2,1)}, u32[]{:S(2)}, u32[]{:S(2)}) %collective-permute-start.1) | collective-permute-done | bytes 405536 | tf_op jit(solution)/shard_map/ppermute | solution.py:104
  53.0 20.0 %collective-permute-done.5.refs_7_.refs_9_ = bf16[192,2560]{1,0:T(8,128)(2,1)} collective-permute-done((bf16[192,2560]{1,0:T(8,128)(2,1)S(1)}, bf16[192,2560]{1,0:T(8,128)(2,1)}, u32[]{:S(2)}, u32[]{:S(2)}) %collective-permute-start.5) | collective-permute-done | bytes 983072 | tf_op jit(solution)/shard_map/ppermute | solution.py:104
  73.1 23.0 %collective-permute-done.4.refs_6_.refs_8_ = bf16[192,2560]{1,0:T(8,128)(2,1)} collective-permute-done((bf16[192,2560]{1,0:T(8,128)(2,1)S(1)}, bf16[192,2560]{1,0:T(8,128)(2,1)}, u32[]{:S(2)}, u32[]{:S(2)}) %collective-permute-start.4) | collective-permute-done | bytes 983072 | tf_op jit(solution)/shard_map/ppermute | solution.py:104
  117.1 8.2 %shard_map.368 = (bf16[256,1536]{1,0:T(8,128)(2,1)}, bf16[256,1024]{1,0:T(8,128)(2,1)}) custom-call(bf16[256,1536]{1,0:T(8,128)(2,1)} %copy.250.refs_0_, f32[256,1]{1,0:T(8,128)} %copy.251.refs_1_.refs_7_.refs_3_, f32[256,128]{1,0:T(8,128)} %copy.252.refs_2_.refs_8_, f32[256,128]{1,0:T(8,128)} %pad_maximum_fusion.5.refs_3_.refs_9_, ...), custom_call_target="tpu_custom_call" | custom-call | flops 1 | bytes 1 | tf_op jit(solution)/shard_map/pallas_call | solution.py:222
  125.3 5.7 all-to-all-done
  141.6 5.8 gather_fusion.1
  147.4 27.9 %collective-permute-done.12.refs_6_.refs_13_ = bf16[256,1024]{1,0:T(8,128)(2,1)} collective-permute-done((bf16[256,1024]{1,0:T(8,128)(2,1)}, bf16[256,1024]{1,0:T(8,128)(2,1)}, u32[]{:S(2)}, u32[]{:S(2)}) %collective-permute-start.12) | collective-permute-done | bytes 524320 | tf_op jit(solution)/shard_map/ppermute | solution.py:104
  175.3 8.4 %collective-permute-done.11.refs_5_.refs_12_ = bf16[256,1024]{1,0:T(8,128)(2,1)} collective-permute-done((bf16[256,1024]{1,0:T(8,128)(2,1)}, bf16[256,1024]{1,0:T(8,128)(2,1)}, u32[]{:S(2)}, u32[]{:S(2)}) %collective-permute-start.11) | collective-permute-done | bytes 524320 | tf_op jit(solution)/shard_map/ppermute | solution.py:104
  190.9 13.2 %shard_map.369 = (f32[256,1536]{1,0:T(8,128)}, bf16[256,1536]{1,0:T(8,128)(2,1)}, f32[4,2,768]{2,1,0:T(2,128)}) custom-call(bf16[256,1536]{1,0:T(8,128)(2,1)} %get-tuple-element.106.refs_0_.refs_1_, s32[1024,1]{1,0:T(8,128)} %copy.253.refs_1_.refs_5_, s32[1,256]{1,0:T(1,128)} %bitcast.238, bf16[256,1024]{1,0:T(8,128)(2,1)} %get-tuple-element.115.refs_3_.refs_10_, ...), custom_call_target="tpu_custom_call" | custom-call | flops 1 | bytes 1 | tf_op jit(solution)/shard_map/pallas_call | solution.py:292
  221.4 40.4 %collective-permute-done.14 = f32[256,5]{1,0:T(8,128)} collective-permute-done((f32[256,5]{1,0:T(8,128)}, f32[256,5]{1,0:T(8,128)}, u32[]{:S(2)}, u32[]{:S(2)}) %collective-permute-start.14) | collective-permute-done | bytes 5152 | tf_op jit(solution)/shard_map/ppermute | solution.py:104
  273.7 16.5 %shard_map.371 = (bf16[2,1024,512]{2,1,0:T(8,128)(2,1)}, bf16[2,1024,1024]{2,1,0:T(8,128)(2,1)}) custom-call(s32[1]{0:T(128)} %bitcast.34.refs_0_, bf16[1024,1536]{1,0:T(8,128)(2,1)} %bitcast.186, f32[1024,5]{1,0:T(8,128)} %constant_dynamic-update-slice_fusion.1.refs_2_, bf16[2,1536,1536]{2,1,0:T(8,128)(2,1)} %all-gather.3.cloned.1.call-done.refs_3_, ...), custom_call_target="tpu_custom_call" | custom-call | flops 1 | bytes 1 | tf_op jit(solution)/shard_map/pallas_call | solution.py:427
  294.6 16.7 %shard_map.373 = bf16[2,1536,1536]{2,1,0:T(8,128)(2,1)} custom-call(bf16[1536,1024]{1,0:T(8,128)(2,1)} %shard_map.372.refs_0_, bf16[1536,1024]{1,0:T(8,128)(2,1)} %shard_map.370.refs_1_, bf16[2,1024,1024]{2,1,0:T(8,128)(2,1)} %get-tuple-element.127.refs_2_.refs_1_, bf16[2,1024,512]{2,1,0:T(8,128)(2,1)} %get-tuple-element.124.refs_3_.refs_1_, ...), custom_call_target="tpu_custom_call" | custom-call | flops 1 | bytes 1 | tf_op jit(solution)/shard_map/pallas_call | solution.py:508
  312.8 22.0 %shard_map.374 = (bf16[3,1024,512]{2,1,0:T(8,128)(2,1)}, bf16[3,1024,1024]{2,1,0:T(8,128)(2,1)}) custom-call(s32[1]{0:T(128)} %bitcast.34.refs_0_, bf16[1024,1536]{1,0:T(8,128)(2,1)} %bitcast.187, f32[1024,5]{1,0:T(8,128)} %constant_dynamic-update-slice_fusion.1.refs_2_, bf16[3,1536,1536]{2,1,0:T(8,128)(2,1)} %all-gather.5.cloned.1.call-done.refs_3_.refs_4_, ...), custom_call_target="tpu_custom_call" | custom-call | flops 1 | bytes 1 | tf_op jit(solution)/shard_map/pallas_call | solution.py:427
  334.8 24.0 %shard_map.375 = (bf16[256,1536]{1,0:T(8,128)(2,1)}, bf16[256,1536]{1,0:T(8,128)(2,1)}, bf16[256,1536]{1,0:T(8,128)(2,1)}, bf16[256,1536]{1,0:T(8,128)(2,1)}) custom-call(s32[1]{0:T(128)} %bitcast.34.refs_0_, bf16[2,1024,1024]{2,1,0:T(8,128)(2,1)} %get-tuple-element.127.refs_2_.refs_1_, bf16[3,1024,1024]{2,1,0:T(8,128)(2,1)} %get-tuple-element.130.refs_2_, ...), custom_call_target="tpu_custom_call" | custom-call | flops 1 | bytes 1 | tf_op jit(solution)/shard_map/pallas_call | solution.py:569
  358.9 23.8 %shard_map.376 = bf16[3,1536,1536]{2,1,0:T(8,128)(2,1)} custom-call(bf16[1536,1024]{1,0:T(8,128)(2,1)} %shard_map.372.refs_0_, bf16[1536,1024]{1,0:T(8,128)(2,1)} %shard_map.370.refs_1_, bf16[3,1024,1024]{2,1,0:T(8,128)(2,1)} %get-tuple-element.130.refs_2_, bf16[3,1024,512]{2,1,0:T(8,128)(2,1)} %get-tuple-element.129.refs_3_.refs_2_, ...), custom_call_target="tpu_custom_call" | custom-call | flops 1 | bytes 1 | tf_op jit(solution)/shard_map/pallas_call | solution.py:508
  382.6 31.3 %reduce-scatter.3.cloned.1.call-done.refs_0_ = bf16[2,192,1536]{2,1,0:T(8,128)(2,1)} async-done(((bf16[2,1536,1536]{2,1,0:T(8,128)(2,1)}), bf16[2,192,1536]{2,1,0:T(8,128)(2,1)}) %reduce-scatter.3.cloned.1.call-update) | async-done | bytes 1179664 | tf_op jit(solution)/shard_map/reduce_scatter | solution.py:898
  416.7 14.5 %shard_map.377 = (bf16[256,1536]{1,0:T(8,128)(2,1)}, bf16[256,1536]{1,0:T(8,128)(2,1)}, bf16[256,1536]{1,0:T(8,128)(2,1)}, bf16[256,1536]{1,0:T(8,128)(2,1)}) custom-call(s32[1]{0:T(128)} %bitcast.34.refs_0_, bf16[2,1024,512]{2,1,0:T(8,128)(2,1)} %get-tuple-element.124.refs_3_.refs_1_, bf16[3,1024,512]{2,1,0:T(8,128)(2,1)} %get-tuple-element.129.refs_3_.refs_2_, ...), custom_call_target="tpu_custom_call" | custom-call | flops 1 | bytes 1 | tf_op jit(solution)/shard_map/pallas_call | solution.py:569
  437.4 14.4 %collective-permute-done.24.refs_7_ = bf16[256,1536]{1,0:T(8,128)(2,1)S(1)} collective-permute-done((bf16[256,1536]{1,0:T(8,128)(2,1)}, bf16[256,1536]{1,0:T(8,128)(2,1)S(1)}, u32[]{:S(2)}, u32[]{:S(2)}) %collective-permute-start.24) | collective-permute-done | bytes 786464 | tf_op jit(solution)/shard_map/ppermute | solution.py:104
  453.6 8.0 %shard_map.378 = (f32[256,1536]{1,0:T(8,128)}, bf16[1536,256]{1,0:T(8,128)(2,1)}, bf16[256,1536]{1,0:T(8,128)(2,1)}, f32[1,1536]{1,0:T(1,128)}) custom-call(f32[256,1]{1,0:T(8,128)} %copy.258.refs_0_, f32[1,1536]{1,0:T(1,128)} %reshape.539.refs_1_, f32[256,1536]{1,0:T(8,128)} %copy-done.3, bf16[256,1536]{1,0:T(8,128)(2,1)} %bitcast.206, ...), custom_call_target="tpu_custom_call" | custom-call | flops 1 | bytes 1 | tf_op jit(solution)/shard_map/pallas_call | solution.py:603
  464.3 20.3 %shard_map.379 = (bf16[256,1536]{1,0:T(8,128)(2,1)}, bf16[4,256,1024]{2,1,0:T(8,128)(2,1)}) custom-call(s32[1]{0:T(128)} %bitcast.43.refs_0_, bf16[256,1536]{1,0:T(8,128)(2,1)} %get-tuple-element.106.refs_0_.refs_1_, bf16[256,1536]{1,0:T(8,128)(2,1)} %get-tuple-element.142.refs_2_, f32[256,1536]{1,0:T(8,128)} %get-tuple-element.143.refs_3_, ...), custom_call_target="tpu_custom_call" | custom-call | flops 1 | bytes 1 | tf_op jit(solution)/shard_map/pallas_call | solution.py:367
  489.9 5.3 shard_map.381
  495.8 5.4 shard_map.380
  504.2 5.1 fusion.5
  512.0 4.8 all-to-all-start.2
  516.8 22.0 %collective-permute-done.29 = bf16[4,48,3200]{2,1,0:T(8,128)(2,1)} collective-permute-done((bf16[4,48,3200]{2,1,0:T(8,128)(2,1)}, bf16[4,48,3200]{2,1,0:T(8,128)(2,1)}, u32[]{:S(2)}, u32[]{:S(2)}) %collective-permute-start.29) | collective-permute-done | bytes 1228832 | tf_op jit(solution)/shard_map/ppermute | solution.py:104
  538.8 27.0 %collective-permute-done.28 = bf16[4,48,3200]{2,1,0:T(8,128)(2,1)} collective-permute-done((bf16[4,48,3200]{2,1,0:T(8,128)(2,1)}, bf16[4,48,3200]{2,1,0:T(8,128)(2,1)}, u32[]{:S(2)}, u32[]{:S(2)}) %collective-permute-start.28) | collective-permute-done | bytes 1228832 | tf_op jit(solution)/shard_map/ppermute | solution.py:104
  570.8 21.2 %all-to-all-done.2.refs_0_ = bf16[4,256,1024]{2,1,0:T(8,128)(2,1)S(1)} async-done(((bf16[4,256,1024]{2,1,0:T(8,128)(2,1)}), bf16[4,256,1024]{2,1,0:T(8,128)(2,1)S(1)}, u32[]{:S(2)}, u32[]{:S(2)}) %all-to-all-start.2) | async-done | bytes 2097184 | tf_op jit(solution)/shard_map/all_to_all | solution.py:125
  617.6 8.3 %shard_map.383 = bf16[256,1536]{1,0:T(8,128)(2,1)} custom-call(s32[32]{0:T(128)} %copy-done.36, bf16[256,1536]{1,0:T(8,128)(2,1)} %get-tuple-element.146.refs_3_.refs_1_, bf16[256,1024]{1,0:T(8,128)(2,1)} %get-tuple-element.161.refs_2_, f32[256,1]{1,0:T(8,128)} %copy.251.refs_1_.refs_7_.refs_3_, bf16[256,1536]{1,0:T(8,128)(2,1)} %bitcast.197, ...), custom_call_target="tpu_custom_call" | custom-call | flops 1 | bytes 1 | tf_op jit(solution)/shard_map/pallas_call | solution.py:704
  626.0 8.3 %collective-permute-done.35 = bf16[4,48,1024]{2,1,0:T(8,128)(2,1)S(1)} collective-permute-done((bf16[4,48,1024]{2,1,0:T(8,128)(2,1)S(1)}, bf16[4,48,1024]{2,1,0:T(8,128)(2,1)S(1)}, u32[]{:S(2)}, u32[]{:S(2)}) %collective-permute-start.35) | collective-permute-done | bytes 393248 | tf_op jit(solution)/shard_map/ppermute | solution.py:104
  635.7 7.6 %shard_map.384 = (f32[5,192,1024]{2,1,0:T(8,128)}, f32[5,192,1024]{2,1,0:T(8,128)}, f32[5,192,1024]{2,1,0:T(8,128)}, f32[5,512,192]{2,1,0:T(8,128)}, f32[5,512,192]{2,1,0:T(8,128)}, /*index=5*/f32[5,512,192]{2,1,0:T(8,128)}) custom-call(bf16[2,192,1536]{2,1,0:T(8,128)(2,1)} %reduce-scatter.3.cloned.1.call-done.refs_0_, f32[5,192,1024]{2,1,0:T(8,128)} %refs_1_.3, ...), custom_call_target="tpu_custom_call" | custom-call | flops 1 | bytes 1 | tf_op jit(solution)/shard_map/pallas_call | solution.py:731
  643.3 11.5 %shard_map.385 = (f32[5,192,1024]{2,1,0:T(8,128)}, f32[5,192,1024]{2,1,0:T(8,128)}, f32[5,192,1024]{2,1,0:T(8,128)}, f32[5,512,192]{2,1,0:T(8,128)}, f32[5,512,192]{2,1,0:T(8,128)}, /*index=5*/f32[5,512,192]{2,1,0:T(8,128)}) custom-call(bf16[3,192,1536]{2,1,0:T(8,128)(2,1)} %reduce-scatter.5., ...), custom_call_target="tpu_custom_call", output_to_operand_aliasing={{0}: (7, {}), {1}: (8, {}), {2}: (9, {}), {3}: (10, {}), {4... | custom-call | flops 1 | bytes 1 | tf_op jit(solution)/shard_map/pallas_call | solution.py:731
  (282 shorter events, 169.8 us)
Async XLA Ops:
  7.2 266.5 %all-gather.3.cloned.1.call-start = ((), (), s32[]{:S(2)}) async-start(), calls=%async_computation.5 | async-start | bytes 10616832 | tf_op jit(solution)/shard_map/all_gather | solution.py:810
  13.1 28.1 %collective-permute-start.2 = (bf16[48,4224]{1,0:T(8,128)(2,1)}, bf16[48,4224]{1,0:T(8,128)(2,1)}, u32[]{:S(2)}, u32[]{:S(2)}) collective-permute-start(bf16[48,4224]{1,0:T(8,128)(2,1)} %pad_maximum_fusion.4), channel_id=1, source_target_pairs={{0,6},{2,4},{4,2},{6,0},{1,7},{3,5},{5,3},{7,1},{8,14},{10,12},{12... | collective-permute-start | bytes 1216520 | tf_op jit(solution)/shard_map/ppermute | solution.py:104
  14.4 34.4 %collective-permute-start.1 = (bf16[48,4224]{1,0:T(8,128)(2,1)}, bf16[48,4224]{1,0:T(8,128)(2,1)}, u32[]{:S(2)}, u32[]{:S(2)}) collective-permute-start(bf16[48,4224]{1,0:T(8,128)(2,1)} %pad_maximum_fusion.4), channel_id=1, source_target_pairs={{0,4},{2,6},{4,0},{6,2},{1,5},{3,7},{5,1},{7,3},{8,12},{10,14},{12... | collective-permute-start | bytes 1216520 | tf_op jit(solution)/shard_map/ppermute | solution.py:104
  15.4 33.4 %collective-permute-start = (bf16[48,4224]{1,0:T(8,128)(2,1)}, bf16[48,4224]{1,0:T(8,128)(2,1)}, u32[]{:S(2)}, u32[]{:S(2)}) collective-permute-start(bf16[48,4224]{1,0:T(8,128)(2,1)} %pad_maximum_fusion.4), channel_id=1, source_target_pairs={{0,2},{2,0},{4,6},{6,4},{1,3},{3,1},{5,7},{7,5},{8,10},{10,8},{12,... | collective-permute-start | bytes 1216520 | tf_op jit(solution)/shard_map/ppermute | solution.py:104
  52.5 43.6 %collective-permute-start.4 = (bf16[192,2560]{1,0:T(8,128)(2,1)S(1)}, bf16[192,2560]{1,0:T(8,128)(2,1)}, u32[]{:S(2)}, u32[]{:S(2)}) collective-permute-start(bf16[192,2560]{1,0:T(8,128)(2,1)S(1)} %slice.149.refs_4_.refs_6_), channel_id=1, source_target_pairs={{0,16},{8,24},{16,0},{24,8},{1,17},{9,25},{17,1},{25,9},{2,18},{10... | collective-permute-start | bytes 2949128 | tf_op jit(solution)/shard_map/ppermute | solution.py:104
  52.7 43.4 %collective-permute-start.3 = (bf16[192,2560]{1,0:T(8,128)(2,1)S(1)}, bf16[192,2560]{1,0:T(8,128)(2,1)}, u32[]{:S(2)}, u32[]{:S(2)}) collective-permute-start(bf16[192,2560]{1,0:T(8,128)(2,1)S(1)} %slice.149.refs_4_.refs_6_), channel_id=1, source_target_pairs={{0,8},{8,0},{16,24},{24,16},{1,9},{9,1},{17,25},{25,17},{2,10},{10... | collective-permute-start | bytes 2949128 | tf_op jit(solution)/shard_map/ppermute | solution.py:104
  97.7 33.2 %all-to-all-start = ((bf16[4,192,1664]{2,1,0:T(8,128)(2,1)}), bf16[4,192,1664]{2,1,0:T(8,128)(2,1)S(1)}, u32[]{:S(2)}, u32[]{:S(2)}) async-start(bf16[4,192,1664]{2,1,0:T(8,128)(2,1)} %broadcast_in_dim.33), calls=%async_computation | async-start | bytes 5111808 | tf_op jit(solution)/shard_map/all_to_all | solution.py:125
  101.5 211.3 %all-gather.5.cloned.1.call-start = ((), (), s32[]{:S(2)}) async-start(), calls=%async_computation.6 | async-start | bytes 15925248 | tf_op jit(solution)/shard_map/all_gather | solution.py:810
  132.4 42.9 %collective-permute-start.12 = (bf16[256,1024]{1,0:T(8,128)(2,1)}, bf16[256,1024]{1,0:T(8,128)(2,1)}, u32[]{:S(2)}, u32[]{:S(2)}) collective-permute-start(bf16[256,1024]{1,0:T(8,128)(2,1)} %get-tuple-element.115.refs_3_.refs_10_), channel_id=1, source_target_pairs={{0,6},{2,4},{4,2},{6,0},{1,7},{3,5},{5,3},{7,1},{8,14},{10,12},{12... | collective-permute-start | bytes 1572872 | tf_op jit(solution)/shard_map/ppermute | solution.py:104
  132.9 50.9 %collective-permute-start.11 = (bf16[256,1024]{1,0:T(8,128)(2,1)}, bf16[256,1024]{1,0:T(8,128)(2,1)}, u32[]{:S(2)}, u32[]{:S(2)}) collective-permute-start(bf16[256,1024]{1,0:T(8,128)(2,1)} %get-tuple-element.115.refs_3_.refs_10_), channel_id=1, source_target_pairs={{0,4},{2,6},{4,0},{6,2},{1,5},{3,7},{5,1},{7,3},{8,12},{10,14},{12... | collective-permute-start | bytes 1572872 | tf_op jit(solution)/shard_map/ppermute | solution.py:104
  136.9 46.9 %collective-permute-start.10 = (bf16[256,1024]{1,0:T(8,128)(2,1)}, bf16[256,1024]{1,0:T(8,128)(2,1)}, u32[]{:S(2)}, u32[]{:S(2)}) collective-permute-start(bf16[256,1024]{1,0:T(8,128)(2,1)} %get-tuple-element.115.refs_3_.refs_10_), channel_id=1, source_target_pairs={{0,2},{2,0},{4,6},{6,4},{1,3},{3,1},{5,7},{7,5},{8,10},{10,8},{12,... | collective-permute-start | bytes 1572872 | tf_op jit(solution)/shard_map/ppermute | solution.py:104
  185.8 81.7 %all-to-all-start.1 = ((bf16[4,256,1536]{2,1,0:T(8,128)(2,1)}), bf16[4,256,1536]{2,1,0:T(8,128)(2,1)S(1)}, u32[]{:S(2)}, u32[]{:S(2)}) async-start(bf16[4,256,1536]{2,1,0:T(8,128)(2,1)} %broadcast_in_dim.35), calls=%async_computation.1 | async-start | bytes 6291456 | tf_op jit(solution)/shard_map/all_to_all | solution.py:125
  189.5 224.4 %reduce-scatter.3.cloned.1.call-start = ((), (), s32[]{:S(2)}) async-start(), calls=%async_computation.7 | async-start | bytes 10616832 | tf_op jit(solution)/shard_map/reduce_scatter | solution.py:898
  211.9 61.7 %collective-permute-start.19 = (bf16[256,1536]{1,0:T(8,128)(2,1)}, bf16[256,1536]{1,0:T(8,128)(2,1)}, u32[]{:S(2)}, u32[]{:S(2)}) collective-permute-start(bf16[256,1536]{1,0:T(8,128)(2,1)} %multiply_convert_fusion.refs_4_.refs_1_), channel_id=1, source_target_pairs={{0,24},{8,16},{16,8},{24,0},{1,25},{9,17},{17,9},{25,1},{2,26},{10... | collective-permute-start | bytes 2359304 | tf_op jit(solution)/shard_map/ppermute | solution.py:104
  214.2 59.4 %collective-permute-start.18 = (bf16[256,1536]{1,0:T(8,128)(2,1)}, bf16[256,1536]{1,0:T(8,128)(2,1)}, u32[]{:S(2)}, u32[]{:S(2)}) collective-permute-start(bf16[256,1536]{1,0:T(8,128)(2,1)} %multiply_convert_fusion.refs_4_.refs_1_), channel_id=1, source_target_pairs={{0,16},{8,24},{16,0},{24,8},{1,17},{9,25},{17,1},{25,9},{2,18},{10... | collective-permute-start | bytes 2359304 | tf_op jit(solution)/shard_map/ppermute | solution.py:104
  214.5 59.1 %collective-permute-start.17 = (bf16[256,1536]{1,0:T(8,128)(2,1)}, bf16[256,1536]{1,0:T(8,128)(2,1)}, u32[]{:S(2)}, u32[]{:S(2)}) collective-permute-start(bf16[256,1536]{1,0:T(8,128)(2,1)} %multiply_convert_fusion.refs_4_.refs_1_), channel_id=1, source_target_pairs={{0,8},{8,0},{16,24},{24,16},{1,9},{9,1},{17,25},{25,17},{2,10},{10... | collective-permute-start | bytes 2359304 | tf_op jit(solution)/shard_map/ppermute | solution.py:104
  216.1 45.7 %collective-permute-start.14 = (f32[256,5]{1,0:T(8,128)}, f32[256,5]{1,0:T(8,128)}, u32[]{:S(2)}, u32[]{:S(2)}) collective-permute-start(f32[256,5]{1,0:T(8,128)} %bitcast.40), channel_id=1, source_target_pairs={{0,8},{8,0},{16,24},{24,16},{1,9},{9,1},{17,25},{25,17},{2,10},{10... | collective-permute-start | bytes 15368 | tf_op jit(solution)/shard_map/ppermute | solution.py:104
  217.6 46.8 %collective-permute-start.15 = (f32[256,5]{1,0:T(8,128)S(1)}, f32[256,5]{1,0:T(8,128)S(1)}, u32[]{:S(2)}, u32[]{:S(2)}) collective-permute-start(f32[256,5]{1,0:T(8,128)S(1)} %bitcast.235), channel_id=1, source_target_pairs={{0,16},{8,24},{16,0},{24,8},{1,17},{9,25},{17,1},{25,9},{2,18},{10... | collective-permute-start | bytes 15368 | tf_op jit(solution)/shard_map/ppermute | solution.py:104
  311.3 332.0 %reduce-scatter.5.cloned.1.call-start = ((), (), s32[]{:S(2)}) async-start(), calls=%async_computation.8 | async-start | bytes 15925248 | tf_op jit(solution)/shard_map/reduce_scatter | solution.py:898
  415.2 36.6 %collective-permute-start.24 = (bf16[256,1536]{1,0:T(8,128)(2,1)}, bf16[256,1536]{1,0:T(8,128)(2,1)S(1)}, u32[]{:S(2)}, u32[]{:S(2)}) collective-permute-start(bf16[256,1536]{1,0:T(8,128)(2,1)} %get-tuple-element.133), channel_id=1, source_target_pairs={{0,16},{8,24},{16,0},{24,8},{1,17},{9,25},{17,1},{25,9},{2,18},{10... | collective-permute-start | bytes 2359304 | tf_op jit(solution)/shard_map/ppermute | solution.py:104
  416.4 35.4 %collective-permute-start.25 = (bf16[256,1536]{1,0:T(8,128)(2,1)}, bf16[256,1536]{1,0:T(8,128)(2,1)S(1)}, u32[]{:S(2)}, u32[]{:S(2)}) collective-permute-start(bf16[256,1536]{1,0:T(8,128)(2,1)} %get-tuple-element.134), channel_id=1, source_target_pairs={{0,24},{8,16},{16,8},{24,0},{1,25},{9,17},{17,9},{25,1},{2,26},{10... | collective-permute-start | bytes 2359304 | tf_op jit(solution)/shard_map/ppermute | solution.py:104
  431.2 53.5 %collective-permute-start.20 = (bf16[256,1536]{1,0:T(8,128)(2,1)}, bf16[256,1536]{1,0:T(8,128)(2,1)S(1)}, u32[]{:S(2)}, u32[]{:S(2)}) collective-permute-start(bf16[256,1536]{1,0:T(8,128)(2,1)} %get-tuple-element.138), channel_id=1, source_target_pairs={{0,8},{8,0},{16,24},{24,16},{1,9},{9,1},{17,25},{25,17},{2,10},{10... | collective-permute-start | bytes 2359304 | tf_op jit(solution)/shard_map/ppermute | solution.py:104
  432.4 53.1 %collective-permute-start.21 = (bf16[256,1536]{1,0:T(8,128)(2,1)}, bf16[256,1536]{1,0:T(8,128)(2,1)}, u32[]{:S(2)}, u32[]{:S(2)}) collective-permute-start(bf16[256,1536]{1,0:T(8,128)(2,1)} %get-tuple-element.139), channel_id=1, source_target_pairs={{0,16},{8,24},{16,0},{24,8},{1,17},{9,25},{17,1},{25,9},{2,18},{10... | collective-permute-start | bytes 2359304 | tf_op jit(solution)/shard_map/ppermute | solution.py:104
  433.9 51.6 %collective-permute-start.22 = (bf16[256,1536]{1,0:T(8,128)(2,1)}, bf16[256,1536]{1,0:T(8,128)(2,1)}, u32[]{:S(2)}, u32[]{:S(2)}) collective-permute-start(bf16[256,1536]{1,0:T(8,128)(2,1)} %get-tuple-element.140), channel_id=1, source_target_pairs={{0,24},{8,16},{16,8},{24,0},{1,25},{9,17},{17,9},{25,1},{2,26},{10... | collective-permute-start | bytes 2359304 | tf_op jit(solution)/shard_map/ppermute | solution.py:104
  509.3 29.5 %collective-permute-start.29 = (bf16[4,48,3200]{2,1,0:T(8,128)(2,1)}, bf16[4,48,3200]{2,1,0:T(8,128)(2,1)}, u32[]{:S(2)}, u32[]{:S(2)}) collective-permute-start(bf16[4,48,3200]{2,1,0:T(8,128)(2,1)} %get-tuple-element.308), channel_id=1, source_target_pairs={{0,24},{8,16},{16,8},{24,0},{1,25},{9,17},{17,9},{25,1},{2,26},{10... | collective-permute-start | bytes 3686408 | tf_op jit(solution)/shard_map/ppermute | solution.py:104
  510.4 55.4 %collective-permute-start.28 = (bf16[4,48,3200]{2,1,0:T(8,128)(2,1)}, bf16[4,48,3200]{2,1,0:T(8,128)(2,1)}, u32[]{:S(2)}, u32[]{:S(2)}) collective-permute-start(bf16[4,48,3200]{2,1,0:T(8,128)(2,1)} %get-tuple-element.309), channel_id=1, source_target_pairs={{0,16},{8,24},{16,0},{24,8},{1,17},{9,25},{17,1},{25,9},{2,18},{10... | collective-permute-start | bytes 3686408 | tf_op jit(solution)/shard_map/ppermute | solution.py:104
  510.9 54.9 %collective-permute-start.27 = (bf16[4,48,3200]{2,1,0:T(8,128)(2,1)}, bf16[4,48,3200]{2,1,0:T(8,128)(2,1)}, u32[]{:S(2)}, u32[]{:S(2)}) collective-permute-start(bf16[4,48,3200]{2,1,0:T(8,128)(2,1)} %get-tuple-element.310), channel_id=1, source_target_pairs={{0,8},{8,0},{16,24},{24,16},{1,9},{9,1},{17,25},{25,17},{2,10},{10... | collective-permute-start | bytes 3686408 | tf_op jit(solution)/shard_map/ppermute | solution.py:104
  512.0 80.0 %all-to-all-start.2 = ((bf16[4,256,1024]{2,1,0:T(8,128)(2,1)}), bf16[4,256,1024]{2,1,0:T(8,128)(2,1)S(1)}, u32[]{:S(2)}, u32[]{:S(2)}) async-start(bf16[4,256,1024]{2,1,0:T(8,128)(2,1)} %get-tuple-element.151), calls=%async_computation.3 | async-start | bytes 4194304 | tf_op jit(solution)/shard_map/all_to_all | solution.py:125
  607.7 47.1 %collective-permute-start.33 = (bf16[48,3200]{1,0:T(8,128)(2,1)}, bf16[48,3200]{1,0:T(8,128)(2,1)}, u32[]{:S(2)}, u32[]{:S(2)}) collective-permute-start(bf16[48,3200]{1,0:T(8,128)(2,1)} %get-tuple-element.324), channel_id=1, source_target_pairs={{0,6},{2,4},{4,2},{6,0},{1,7},{3,5},{5,3},{7,1},{8,14},{10,12},{12... | collective-permute-start | bytes 921608 | tf_op jit(solution)/shard_map/ppermute | solution.py:104
  609.2 47.4 %collective-permute-start.32 = (bf16[48,3200]{1,0:T(8,128)(2,1)}, bf16[48,3200]{1,0:T(8,128)(2,1)}, u32[]{:S(2)}, u32[]{:S(2)}) collective-permute-start(bf16[48,3200]{1,0:T(8,128)(2,1)} %get-tuple-element.325), channel_id=1, source_target_pairs={{0,4},{2,6},{4,0},{6,2},{1,5},{3,7},{5,1},{7,3},{8,12},{10,14},{12... | collective-permute-start | bytes 921608 | tf_op jit(solution)/shard_map/ppermute | solution.py:104
  625.9 30.6 %collective-permute-start.31 = (bf16[48,3200]{1,0:T(8,128)(2,1)S(1)}, bf16[48,3200]{1,0:T(8,128)(2,1)}, u32[]{:S(2)}, u32[]{:S(2)}) collective-permute-start(bf16[48,3200]{1,0:T(8,128)(2,1)S(1)} %copy-done.25), channel_id=1, source_target_pairs={{0,2},{2,0},{4,6},{6,4},{1,3},{3,1},{5,7},{7,5},{8,10},{10,8},{12,... | collective-permute-start | bytes 921608 | tf_op jit(solution)/shard_map/ppermute | solution.py:104
  634.6 23.4 %collective-permute-start.39 = (bf16[48,1024]{1,0:T(8,128)(2,1)S(1)}, bf16[48,1024]{1,0:T(8,128)(2,1)S(1)}, u32[]{:S(2)}, u32[]{:S(2)}) collective-permute-start(bf16[48,1024]{1,0:T(8,128)(2,1)S(1)} %get-tuple-element.330), channel_id=1, source_target_pairs={{0,6},{2,4},{4,2},{6,0},{1,7},{3,5},{5,3},{7,1},{8,14},{10,12},{12... | collective-permute-start | bytes 294920 | tf_op jit(solution)/shard_map/ppermute | solution.py:104
  (55 other events, 546.3 us)
Sparse Core Ops, SparseCore 0:
  50.3 113.9 all-gather.2
  183.9 128.8 all-gather.4
  315.1 98.7 reduce-scatter.2
  416.1 187.6 reduce-scatter.4
where the time goes:
time: 695 us; the launch traced here: 684 us
  waiting for transfers between devices  285 us (41%)
  Pallas kernels  219 us (32%)
  local copies, waits for them, and re-layouts  63.3 us (9%)
  starting transfers between devices  54.8 us (8%)
  other arithmetic  40.3 us (6%)
  between operations  15.1 us (2%)
  matrix products  7.87 us (1%)
    ppermute x40, waiting for transfers between devices, swap(): return lax.ppermute(block, axis, [(i, i ^ step) for i in range(count)])  225 us
    ppermute x40, starting transfers between devices, swap(): return lax.ppermute(block, axis, [(i, i ^ step) for i in range(count)])  42.2 us
    pallas_call x2, Pallas kernels, expert_weight_grads(): call(functools.partial(weight_grad_body, sizes), (sum(sizes), width // bl...  40.5 us
    pallas_call x2, Pallas kernels, combine(): call(functools.partial(combine_body, sizes), (sum(sizes),), [SCALAR] + pa...  38.5 us
    pallas_call x2, Pallas kernels, expert_hidden(): call(functools.partial(hidden_body, len(parts), first), (experts, tokens...  38.5 us
    reduce_scatter x2, waiting for transfers between devices, to_owners(): lax.psum_scatter(grads, ('context', 'dp'), scatter_dimension=1, tiled=True)  31.3 us
    all_to_all x3, waiting for transfers between devices, trade(): return lax.all_to_all(blocks, axis, split_axis=0, concat_axis=0, tiled=True)  26.8 us
    unnamed x88, local copies, waits for them, and re-layouts  21.5 us
  transfers between devices with their start and end apart: 47, of which 21 were waited for; matrix products, arithmetic and copies ran while one was open for 12% of the time, Pallas kernels for 32%

commit v1 on v0

--- a/solution.py
+++ b/solution.py
@@ -133,32 +133,6 @@
     return joined
 
 
-class OwnerSum:
-    def __init__(self, own, other, shape):
-        self.own = own.reshape(shape)
-        self.came = swap(other, "dp", 1).reshape(shape)
-
-    def spread_experts(self, *others):
-        came = after(self.came, *others)
-        both = [
-            (self.own[k].astype(wide) + came[k].astype(wide)).astype(low)
-            for k in range(self.own.shape[0])
-        ]
-        self.parts = [both[0]] + [swap(both[k], "expert", k) for k in range(1, len(both))]
-        return both
-
-    def spread_contexts(self, *others):
-        parts = all_after(self.parts, *others)
-        total = functools.reduce(jnp.add, [part.astype(wide) for part in parts])
-        column = [total[k].astype(low) for k in range(1, total.shape[0])]
-        self.parts = [total[0]] + [swap(part, "context", k + 1) for k, part in enumerate(column)]
-        return column
-
-    def finish(self, *others):
-        parts = all_after(self.parts, *others)
-        return functools.reduce(jnp.add, [part.astype(wide) for part in parts])
-
-
 def call(body, grid, in_specs, out_specs, out_shape, scratch=(), aliases=None):
     order = pl.BlockSpec(TOKEN, lambda *_: (0, 0))
 
@@ -181,6 +155,78 @@
 
 def token(*others):
     return lax.optimization_barrier((jnp.zeros(TOKEN, wide), *others))[0]
+
+
+def halves_body(own_ref, came_ref, *out_refs):
+    total = own_ref[...].astype(wide) + came_ref[...].astype(wide)
+    rows = out_refs[0].shape[0]
+    for k, out_ref in enumerate(out_refs):
+        out_ref[...] = total[k * rows : (k + 1) * rows, :].astype(low)
+
+
+def add_halves(own, came, parts, order):
+    rows, columns = own.shape
+    block = max(b for b in (128, 256, 512, 640) if columns % b == 0)
+    spec = pl.BlockSpec((rows, block), lambda j: (0, j))
+    out = pl.BlockSpec((rows // parts, block), lambda j: (0, j))
+    return call(
+        halves_body,
+        (columns // block,),
+        [spec, spec],
+        [out] * parts,
+        [jax.ShapeDtypeStruct((rows // parts, columns), low)] * parts,
+    )(own, came, order)
+
+
+def parts_body(count, *refs):
+    part_refs, out_refs = refs[:count], refs[count:]
+    total = functools.reduce(jnp.add, [ref[...].astype(wide) for ref in part_refs])
+    rows = out_refs[0].shape[0]
+    for k, out_ref in enumerate(out_refs):
+        out_ref[...] = total[k * rows : (k + 1) * rows, :].astype(out_ref.dtype)
+
+
+def add_parts(parts, cuts, order):
+    rows, columns = parts[0].shape
+    block = max(b for b in (128, 256, 512, 640) if columns % b == 0)
+    spec = pl.BlockSpec((rows, block), lambda j: (0, j))
+    out = pl.BlockSpec((rows // cuts, block), lambda j: (0, j))
+    shape = (rows // cuts, columns)
+    return call(
+        functools.partial(parts_body, len(parts)),
+        (columns // block,),
+        [spec] * len(parts),
+        [out] * cuts,
+        [jax.ShapeDtypeStruct(shape, wide)] + [jax.ShapeDtypeStruct(shape, low)] * (cuts - 1),
+    )(*parts, order)
+
+
+class OwnerSum:
+    def __init__(self, own, other, owners, contexts):
+        self.own = own
+        self.came = swap(other, "dp", 1)
+        self.owners, self.contexts = owners, contexts
+
+    def spread_experts(self, *others):
+        if self.own.shape[0] // self.owners // self.contexts % 16 == 0:
+            both = add_halves(self.own, self.came, self.owners, token(*others))
+        else:
+            came = after(self.came, *others)
+            total = (self.own.astype(wide) + came.astype(wide)).astype(low)
+            both = list(total.reshape(self.owners, -1, total.shape[1]))
+        self.parts = [both[0]] + [swap(both[k], "expert", k) for k in range(1, len(both))]
+        return both
+
+    def spread_contexts(self, *others):
+        if self.parts[0].shape[0] // self.contexts % 16 == 0:
+            total = add_parts(self.parts, self.contexts, token(*others))
+        else:
+            parts = all_after(self.parts, *others)
+            total = functools.reduce(jnp.add, [part.astype(wide) for part in parts])
+            total = total.reshape(self.contexts, -1, total.shape[1])
+            total = [total[0]] + [part.astype(low) for part in total[1:]]
+        self.parts = [total[0]] + [swap(part, "context", k) for k, part in enumerate(total) if k]
+        return total[1:]
 
 
 def turn(vals, cosine, sine):
@@ -585,7 +631,8 @@
         grad = functools.reduce(jnp.add, [ref[...].astype(wide) for ref in part_refs])
         scale = scale_ref[...]
         unit = middle_ref[...] * scale
-        gain_grad_ref[...] = jnp.sum(grad * unit, axis=0, keepdims=True)
+        gain = jnp.sum((grad * unit).T, axis=1, keepdims=True)
+        gain_grad_ref[...] = jnp.broadcast_to(gain, gain_grad_ref.shape).astype(low)
         grad = grad * gain_ref[...]
         mean = jnp.mean(grad * unit, axis=1, keepdims=True)
         grad = cotangent_ref[...].astype(wide) + scale * (grad - unit * mean)
@@ -615,39 +662,56 @@
             whole((tokens, width)),
             whole((width, tokens)),
             pl.BlockSpec((tokens, block), lambda j: (0, j)),
-            whole((1, width)),
+            whole((width, LANES)),
         ],
         [
             jax.ShapeDtypeStruct((tokens, width), wide),
             jax.ShapeDtypeStruct((width, tokens), low),
             jax.ShapeDtypeStruct((tokens, QUERY_WIDTH), low),
-            jax.ShapeDtypeStruct((1, width), wide),
+            jax.ShapeDtypeStruct((width, LANES), low),
         ],
         scratch=[pltpu.VMEM((tokens, width), low)],
     )(scale, gain, middle, cotangent, output_pack, *parts, order)
 
 
-def outer_body(input_ref, proj_ref, gain_ref, query_ref, attended_ref, out_ref):
+def outer_body(rows, first, place_ref, input_ref, proj_ref, gain_ref, query_ref, attended_ref,
+               out_ref, picked_ref):
     out_ref[:, :QUERY_WIDTH] = dot_nn(input_ref[...], query_ref[...]).astype(low)
-    out_ref[:, QUERY_WIDTH : 2 * QUERY_WIDTH] = dot_nn(proj_ref[...], attended_ref[...]).astype(low)
-    out_ref[:, 2 * QUERY_WIDTH :] = jnp.broadcast_to(
-        gain_ref[...], (gain_ref.shape[0], LANES)
-    ).astype(low)
-
-
-def outer_grads(half, cores, input_turned, proj_turned, gain_grads, grad_query, attended, order):
+    if rows:
+        for i in range(out_ref.shape[0] // rows):
+            start = pl.multiple_of(place_ref[first + i] * rows, rows)
+            part = slice(i * rows, (i + 1) * rows)
+            picked_ref[part, :] = proj_ref[pl.ds(start, rows), :]
+            out_ref[part, 2 * QUERY_WIDTH :] = gain_ref[pl.ds(start, rows), :]
+    else:
+        picked_ref[...] = proj_ref[...]
+        out_ref[:, 2 * QUERY_WIDTH :] = gain_ref[...]
+    out_ref[:, QUERY_WIDTH : 2 * QUERY_WIDTH] = dot_nn(picked_ref[...], attended_ref[...]).astype(low)
+
+
+def outer_grads(half, cores, place, input_turned, proj_turned, gain_turned, grad_query, attended, order):
     width, tokens = input_turned.shape
     rows = width // cores
+    slice_rows = width // place.shape[0]
     part = lambda columns: pl.BlockSpec((rows, columns), lambda i: (half, 0))
+    inside = slice_rows % 16 == 0
+    every = lambda columns: pl.BlockSpec((width, columns), lambda i: (0, 0))
+    if not inside:
+        pick = lambda array: jnp.take(
+            array.reshape(place.shape[0], slice_rows, -1), place, axis=0, mode="clip"
+        ).reshape(array.shape)
+        proj_turned, gain_turned = pick(proj_turned), pick(gain_turned)
+        every = part
     whole = pl.BlockSpec((tokens, QUERY_WIDTH), lambda i: (0, 0))
     columns = 2 * QUERY_WIDTH + LANES
     return call(
-        outer_body,
+        functools.partial(outer_body, slice_rows if inside else 0, half * (place.shape[0] // cores)),
         (1,),
-        [part(tokens), part(tokens), part(1), whole, whole],
+        [SCALAR, part(tokens), every(tokens), every(LANES), whole, whole],
         pl.BlockSpec((rows, columns), lambda i: (0, 0)),
         jax.ShapeDtypeStruct((rows, columns), low),
-    )(input_turned, proj_turned, gain_grads, grad_query, attended, order)
+        scratch=[pltpu.VMEM((rows, tokens), low)],
+    )(place, input_turned, proj_turned, gain_turned, grad_query, attended, order)
 
 
 def kv_body(parts_ref, scale_ref, cos_ref, sin_ref, input_ref, grad_ref, *out_refs):
@@ -717,7 +781,7 @@
     split = expand[0].shape[2]
     for arrays, grad, rate, out_refs in (
         (expand, grads[:, :split], rate_expand, refs[:3]),
-        (contract, grads[:, split:].T, rate_contract, refs[3:]),
+        (contract, grads[:, split:], rate_contract, refs[3:]),
     ):
         results = adamw(*[array[0] for array in arrays], grad, rate, decay_rate)
         for out_ref, result in zip(out_refs, results):
@@ -738,6 +802,53 @@
         [jax.ShapeDtypeStruct(array.shape, wide) for array in arrays],
         aliases={1 + len(arrays) + i: i for i in range(len(held))},
     )(grads, *arrays, *held, order)
+
+
+def adam_joined_body(count, query_mat_ref, key_mat_ref, gain_ref, *refs):
+    grads, kv = [
+        functools.reduce(jnp.add, [ref[...].astype(wide) for ref in part])
+        for part in (refs[:count], refs[count : 2 * count])
+    ]
+    refs = refs[2 * count :]
+    joined, output, gains, outs = refs[:3], refs[3:6], refs[6:9], refs[9:]
+    back = lambda grad, mat: lax.dot_general(
+        grad, mat, (((1,), (1,)), ((), ())), precision=lax.Precision.HIGHEST, preferred_element_type=wide
+    )
+    query_mat, key_mat = query_mat_ref[...], key_mat_ref[...]
+    pairs = lambda start: [
+        back(grads[:, start + p * PAIR_WIDTH : start + (p + 1) * PAIR_WIDTH], query_mat)
+        for p in range(PAIRS)
+    ]
+    keys = [back(kv[:, 2 * p * LANES : (2 * p + 1) * LANES], key_mat) for p in range(PAIRS)]
+    values = [back(kv[:, (2 * p + 1) * LANES : (2 * p + 2) * LANES], key_mat) for p in range(PAIRS)]
+    unit_grad = jnp.concatenate([*pairs(0), *keys, *values], axis=1)
+    low_weight = joined[0][...].astype(low).astype(wide)
+    gain_one = jnp.sum(low_weight * unit_grad, axis=1, keepdims=True)
+    gain_two = grads[:, 2 * QUERY_WIDTH : 2 * QUERY_WIDTH + 1]
+    output_grad = jnp.concatenate(pairs(QUERY_WIDTH), axis=1)
+    joined_grad = gain_ref[...] * unit_grad
+    gains_grad = jnp.concatenate([gain_one, gain_two], axis=1)
+    for arrays, grad, rate, decay, out_refs in (
+        (joined, joined_grad, rate_joined, decay_rate, outs[:3]),
+        (output, output_grad, rate_output, decay_rate, outs[3:6]),
+        (gains, gains_grad, rate_gains, 0.0, outs[6:]),
+    ):
+        results = adamw(*[array[...] for array in arrays], grad, rate, decay)
+        for out_ref, result in zip(out_refs, results):
+            out_ref[...] = result
+
+
+def adam_joined(gain, query_parts, kv_parts, arrays, order):
+    query_mat, key_mat = order_matrix(GROUPS).astype(wide), order_matrix(1).astype(wide)
+    operands = [query_mat, key_mat, gain, *query_parts, *kv_parts, *arrays]
+    whole = lambda array: pl.BlockSpec(array.shape, lambda i: (0, 0))
+    return call(
+        functools.partial(adam_joined_body, len(query_parts)),
+        (1,),
+        [whole(operand) for operand in operands],
+        [whole(array) for array in arrays],
+        [jax.ShapeDtypeStruct(array.shape, wide) for array in arrays],
+    )(*operands, order)
 
 
 def body(
@@ -805,8 +916,6 @@
         (jnp.concatenate(spread(shard, "context"), axis=0), *expert_low)
     )
     joined_mine = spread(line[:, :columns], "expert")
-    joined_parts = joined_mine + [swap(part, "dp", 1) for part in joined_mine]
-    output_mine = share(after(line[:, columns:], *joined_mine), "expert")
     gather_expert = lambda part: lax.all_gather(part, ("context", "dp"), axis=1, tiled=True)
     expert_full = [gather_expert(expert_low[0])]
 
@@ -834,8 +943,6 @@
         lax.dynamic_index_in_dim(gate_table, own_expert ^ k, axis=1, keepdims=False)
         for k in range(owners)
     ]
-    gate_parts = [gate_sent[0]] + [swap(gate_sent[k], "expert", k) for k in range(1, owners)]
-    gates = in_order(gate_parts, own_expert)
     own = own_expert.reshape(1)
     zero = jnp.zeros((1,), jnp.int32)
 
@@ -861,9 +968,16 @@
     unit_one = resid * scale_one
     input_turned = pick_rows(low_input.T, to_relative)
     input_relative = input_turned.T
+    gate_sent = all_after(gate_sent, line)
+    gate_parts = [gate_sent[0]] + [swap(gate_sent[k], "expert", k) for k in range(1, owners)]
+    joined_mine = [joined_mine[0]] + all_after(
+        joined_mine[1:], cosine, sine, scale_one, input_relative, *gate_sent
+    )
+    joined_parts = joined_mine + [swap(part, "dp", 1) for part in joined_mine]
     query, kv = project(input_relative, scale_one, cosine, sine, joined_parts, token())
     kv_parts = spread(kv, "context")
-    output_mine = after(output_mine, kv)
+    output_mine = share(after(line[:, columns:], kv), "expert")
+    gates = in_order(all_after(gate_parts, kv), own_expert)
     output_parts = [output_mine, swap(output_mine, "dp", 1)]
     out_grads = share(after(cotangent[0], output_mine), "expert").reshape(-1, width)
     output_place = (
@@ -875,7 +989,8 @@
     )
     output_turned = output_pack[:, :QUERY_WIDTH]
     gain_two = output_pack[:, QUERY_WIDTH].astype(wide)[None, :]
-    kv_parts = all_after(kv_parts, output_pack)
+    out_grads_turned = turn_rows(zero, [out_grads], token(output_pack))
+    kv_parts = all_after(kv_parts, output_pack, out_grads_turned, gates)
     kv_parts, later = lax.optimization_barrier((kv_parts, expert_low[1:]))
     expert_full += [gather_expert(part) for part in later]
     attended_wide, attended, logs = attend(
@@ -887,8 +1002,6 @@
     normed_two = (unit_two * gain_two).astype(low)
 
     row_parts = spread(normed_two, "expert")
-    out_grads_turned = turn_rows(zero, [out_grads], token(normed_two))
-
     def grads_of(hidden, back, *others):
         return expert_weight_grads(
             rows_turned, out_grads_turned, [(hidden, back, 0, back.shape[0])], token(*others)
@@ -902,7 +1015,7 @@
 
     cut = bounds[1]
     first_unit = expert_hidden(
-        own, row_parts, out_grads, gates, 0, expert_full[0], token(out_grads_turned)
+        own, row_parts, out_grads, gates, 0, expert_full[0], token()
     )
     rows_turned = turn_rows(own, row_parts, token(first_unit[0]))
     first_grads = grads_of(*first_unit)
@@ -919,36 +1032,34 @@
     )
     mixture_parts = to_tokens(mixture_sent)
 
-    grad_middle, proj_turned, grad_attended, gain_grad_two = norm_back_two(
+    grad_middle, proj_turned, grad_attended, gain_turned = norm_back_two(
         grad_parts, middle, scale_two, gain_two, cotangent[0], output_pack, token(*mixture_sent)
     )
     grad_query, grad_kv = attend_back(
         own_context.reshape(1), query, grad_attended, attended_wide, logs, key_pos[:, None], query_pos[None, :],
         scale_one, cosine, sine, kv_parts, token(grad_attended, first_sum),
     )
-    expert_grads = [first_sum, to_owners(after(second_grads, first_sum))]
+    expert_grads = [first_sum, to_owners(after(second_grads, first_sum, grad_attended))]
     grad_kv_parts = trade(grad_kv, "context")
+
+    def outer(half, *others):
+        return outer_grads(
+            half, cores, to_relative, input_turned, proj_turned, gain_turned, grad_query, attended,
+            token(*others),
+        )
 
     mixture = functools.reduce(
         jnp.add, [part.astype(wide) for part in all_after(mixture_parts, grad_query)]
     )
     output = (middle + mixture).astype(low)
-    relative = (owners, contexts, slice_rows, -1)
-    proj_turned = pick_rows(after(proj_turned, output), to_relative)
-    gain_grads = pick_rows(gain_grad_two.reshape(width, 1), to_relative)
-    other, own_part = [
-        outer_grads(
-            half, cores, input_turned, proj_turned, gain_grads, grad_query, attended, token()
-        )
-        for half in (1, 0)
-    ]
-    query_sum = OwnerSum(own_part, other, relative)
-    latest = query_sum.spread_experts(own_part)
+    other = outer(1, output)
+    query_sum = OwnerSum(outer(0, other), other, owners, contexts)
+    latest = query_sum.spread_experts(query_sum.own)
     latest = query_sum.spread_contexts(*latest)
     own_grad_kv, *kv_parts_sent = kv_grads(
         cores, grad_kv_parts, scale_one, cosine, sine, input_turned, token(*latest)
     )
-    kv_sum = OwnerSum(*kv_parts_sent, relative)
+    kv_sum = OwnerSum(*kv_parts_sent, owners, contexts)
     latest = kv_sum.spread_experts(own_grad_kv)
     if slice_rows % 16 == 0:
         grad_input = input_grads(
@@ -966,35 +1077,24 @@
         ).astype(low)
 
     latest = kv_sum.spread_contexts(grad_input)
-    arrays = [
-        expand_weight, expand_first, expand_second, contract_weight, contract_first, contract_second
-    ]
+    contract_arrays = [contract_weight, contract_first, contract_second]
+    arrays = [expand_weight, expand_first, expand_second]
+    arrays += [jnp.swapaxes(array, 1, 2) for array in contract_arrays]
     expert_new = adam_experts(0, expert_grads[0], arrays, None, token(*latest))
     expert_new = adam_experts(cut, expert_grads[1], arrays, expert_new, token())
-    expand_new, contract_new = expert_new[:3], expert_new[3:]
-    sum_query = query_sum.finish(*latest, expand_new[0])
-    sum_kv = kv_sum.finish(sum_query)
-    sum_output = sum_query[:, QUERY_WIDTH:]
-    sum_joined = jnp.concatenate([sum_query[:, :QUERY_WIDTH], sum_kv], axis=1)
-
-    unit_grads = reorder_columns(sum_joined, back=True)
-    sum_joined = gain_rows[:, :1] * unit_grads
-    sum_gain_one = jnp.sum(joined_low.astype(wide) * unit_grads, axis=1)
-    sum_gains = jnp.stack([sum_gain_one, sum_output[:, QUERY_WIDTH]], axis=0)
-    sum_output_weight = jnp.einsum(
-        "on,dpn->pod",
-        query_mat.astype(wide),
-        sum_output[:, :QUERY_WIDTH].reshape(slice_rows, PAIRS, PAIR_WIDTH),
-        precision=lax.Precision.HIGHEST,
-        preferred_element_type=wide,
-    ).reshape(QUERY_WIDTH, slice_rows)
-    joined_new = adamw(
-        joined_weight, joined_first, joined_second, sum_joined, rate_joined, decay_rate
-    )
-    output_new = adamw(
-        output_weight, output_first, output_second, sum_output_weight, rate_output, decay_rate
-    )
-    gains_new = adamw(norm_gains, gains_first, gains_second, sum_gains, rate_gains, 0.0)
+    expand_new = expert_new[:3]
+    contract_new = [jnp.swapaxes(array, 1, 2) for array in expert_new[3:]]
+    turned = [output_weight, output_first, output_second, norm_gains, gains_first, gains_second]
+    joined_new = adam_joined(
+        gain_rows[:, :1],
+        query_sum.parts,
+        kv_sum.parts,
+        [joined_weight, joined_first, joined_second] + [array.T for array in turned],
+        token(expand_new[0]),
+    )
+    output_new = [array.T for array in joined_new[3:6]]
+    gains_new = [array.T for array in joined_new[6:]]
+    joined_new = joined_new[:3]
     return (
         output.reshape(1, tokens, width),
         grad_input.reshape(1, tokens, width),

time: 695 us -> 715 us (1.029)
  blocking collectives: 0 us -> 33.5 us
  Pallas kernels: 219 us -> 245 us
  local copies, waits for them, and re-layouts: 63.3 us -> 42.8 us
  other arithmetic: 40.3 us -> 23.5 us
    all_to_all x0 -> x1, blocking collectives: none -> 33.5 us  [trade(): return lax.all_to_all(blocks, axis, split_axis=0, concat_axis=0, tiled=True)]
    all_gather x2, waiting for transfers between devices: 1.49 us -> 31.7 us  [body(): lax.all_gather(part, ('context', 'dp'), axis=1, tiled=True)]
    pallas_call x2 -> x7, Pallas kernels: 10.7 us -> 37.7 us  [the longest x2 11 us: outer_grads(): call(functools.partial(outer_body, slice_rows if inside else 0, half * (p...]
    all_to_all x3 -> x2, waiting for transfers between devices: 26.8 us -> 4.34 us  [trade(): return lax.all_to_all(blocks, axis, split_axis=0, concat_axis=0, tiled=True)]
    ppermute x40, waiting for transfers between devices: 225 us -> 209 us  [swap(): return lax.ppermute(block, axis, [(i, i ^ step) for i in range(count)])]
    reduce_scatter x2, waiting for transfers between devices: 31.3 us -> 46.4 us  [to_owners(): lax.psum_scatter(grads, ('context', 'dp'), scatter_dimension=1, tiled=True)]
    unnamed x88 -> x121, local copies, waits for them, and re-layouts: 21.5 us -> 15.8 us
  transfers between devices with their start and end apart: 47 -> 46, of which waited for: 21 -> 20; matrix products, arithmetic and copies ran while one was open for 12% -> 7% of each run, Pallas kernels for 32% -> 33%
where the time goes in v1:
time: 715 us; the launch traced here: 706 us
  waiting for transfers between devices  292 us (41%)
  Pallas kernels  245 us (34%)
  starting transfers between devices  50.6 us (7%)
  local copies, waits for them, and re-layouts  42.8 us (6%)
  blocking collectives  33.5 us (5%)
  other arithmetic  23.5 us (3%)
  between operations  14.8 us (2%)
    ppermute x40, waiting for transfers between devices, swap(): return lax.ppermute(block, axis, [(i, i ^ step) for i in range(count)])  209 us
    reduce_scatter x2, waiting for transfers between devices, to_owners(): lax.psum_scatter(grads, ('context', 'dp'), scatter_dimension=1, tiled=True)  46.4 us
    ppermute x40, starting transfers between devices, swap(): return lax.ppermute(block, axis, [(i, i ^ step) for i in range(count)])  41.7 us
    pallas_call x2, Pallas kernels, expert_weight_grads(): call(functools.partial(weight_grad_body, sizes), (sum(sizes), width // bl...  40.4 us
    pallas_call x2, Pallas kernels, combine(): call(functools.partial(combine_body, sizes), (sum(sizes),), [SCALAR] + pa...  38.7 us
    pallas_call x2, Pallas kernels, expert_hidden(): call(functools.partial(hidden_body, len(parts), first), (experts, tokens...  38.2 us
    all_to_all x1, blocking collectives, trade(): return lax.all_to_all(blocks, axis, split_axis=0, concat_axis=0, tiled=True)  33.5 us
    all_gather x2, waiting for transfers between devices, body(): lax.all_gather(part, ('context', 'dp'), axis=1, tiled=True)  31.7 us
  transfers between devices with their start and end apart: 46, of which 20 were waited for; matrix products, arithmetic and copies ran while one was open for 7% of the time, Pallas kernels for 33%

profile of v1, /device:TPU:9, one launch (start us, length us, event | category | flops | bytes accessed | tf_op | source)
XLA Modules:
  0.0 706.4 jit_solution(17746818746569280839)
XLA Ops:
  19.6 21.4 %collective-permute-done.2 = bf16[48,4224]{1,0:T(8,128)(2,1)S(1)} collective-permute-done((bf16[48,4224]{1,0:T(8,128)(2,1)}, bf16[48,4224]{1,0:T(8,128)(2,1)S(1)}, u32[]{:S(2)}, u32[]{:S(2)}) %collective-permute-start.2) | collective-permute-done | bytes 405536 | tf_op jit(solution)/shard_map/ppermute | solution.py:104
  41.1 7.6 %collective-permute-done.1 = bf16[48,4224]{1,0:T(8,128)(2,1)} collective-permute-done((bf16[48,4224]{1,0:T(8,128)(2,1)}, bf16[48,4224]{1,0:T(8,128)(2,1)}, u32[]{:S(2)}, u32[]{:S(2)}) %collective-permute-start.1) | collective-permute-done | bytes 405536 | tf_op jit(solution)/shard_map/ppermute | solution.py:104
  66.9 8.2 %collective-permute-done.5.refs_7_.refs_9_ = bf16[192,2560]{1,0:T(8,128)(2,1)} collective-permute-done((bf16[192,2560]{1,0:T(8,128)(2,1)S(1)}, bf16[192,2560]{1,0:T(8,128)(2,1)}, u32[]{:S(2)}, u32[]{:S(2)}) %collective-permute-start.5) | collective-permute-done | bytes 983072 | tf_op jit(solution)/shard_map/ppermute | solution.py:104
  75.1 23.0 %collective-permute-done.4.refs_6_.refs_8_ = bf16[192,2560]{1,0:T(8,128)(2,1)} collective-permute-done((bf16[192,2560]{1,0:T(8,128)(2,1)S(1)}, bf16[192,2560]{1,0:T(8,128)(2,1)}, u32[]{:S(2)}, u32[]{:S(2)}) %collective-permute-start.4) | collective-permute-done | bytes 983072 | tf_op jit(solution)/shard_map/ppermute | solution.py:104
  105.9 8.3 %shard_map.368 = (bf16[256,1536]{1,0:T(8,128)(2,1)}, bf16[256,1024]{1,0:T(8,128)(2,1)}) custom-call(bf16[256,1536]{1,0:T(8,128)(2,1)} %copy.136.refs_0_, f32[256,1]{1,0:T(8,128)} %copy.137.refs_1_.refs_7_.refs_3_, f32[256,128]{1,0:T(8,128)} %copy.138.refs_2_.refs_8_, f32[256,128]{1,0:T(8,128)} %pad_maximum_fusion.5.refs_3_.refs_9_, ...), custom_call_target="tpu_custom_call" | custom-call | flops 1 | bytes 1 | tf_op jit(solution)/shard_map/pallas_call | solution.py:268
  114.3 33.5 %all_to_all.15 = bf16[4,192,1664]{2,1,0:T(8,128)(2,1)} all-to-all(bf16[4,192,1664]{2,1,0:T(8,128)(2,1)S(1)} %broadcast_in_dim.35), channel_id=1, replica_groups=mesh['expert'=4,'context'=4,'dp'=2] {'expert'}, dimensions={0} | all-to-all | bytes 5111808 | tf_op jit(solution)/shard_map/all_to_all | solution.py:125
  158.1 36.0 %collective-permute-done.14 = f32[256,5]{1,0:T(8,128)} collective-permute-done((f32[256,5]{1,0:T(8,128)}, f32[256,5]{1,0:T(8,128)}, u32[]{:S(2)}, u32[]{:S(2)}) %collective-permute-start.14) | collective-permute-done | bytes 5152 | tf_op jit(solution)/shard_map/ppermute | solution.py:104
  204.0 5.1 pad_maximum_fusion
  209.1 5.8 gather_fusion.1
  222.9 13.2 %shard_map.370 = (f32[256,1536]{1,0:T(8,128)}, bf16[256,1536]{1,0:T(8,128)(2,1)}, f32[4,2,768]{2,1,0:T(2,128)}) custom-call(bf16[256,1536]{1,0:T(8,128)(2,1)} %get-tuple-element.135.refs_0_.refs_1_, s32[1024,1]{1,0:T(8,128)} %copy.139.refs_1_.refs_5_, s32[1,256]{1,0:T(1,128)} %bitcast.165, bf16[256,1024]{1,0:T(8,128)(2,1)} %get-tuple-element.149.refs_3_.refs_10_, ...), custom_call_target="tpu_custom_call" | custom-call | flops 1 | bytes 1 | tf_op jit(solution)/shard_map/pallas_call | solution.py:338
  244.3 16.6 %collective-permute-done.19.refs_7_.refs_4_ = bf16[256,1536]{1,0:T(8,128)(2,1)S(1)} collective-permute-done((bf16[256,1536]{1,0:T(8,128)(2,1)S(1)}, bf16[256,1536]{1,0:T(8,128)(2,1)S(1)}, u32[]{:S(2)}, u32[]{:S(2)}) %collective-permute-start.19) | collective-permute-done | bytes 786464 | tf_op jit(solution)/shard_map/ppermute | solution.py:104
  261.0 17.1 %collective-permute-done.18.refs_6_.refs_3_ = bf16[256,1536]{1,0:T(8,128)(2,1)S(1)} collective-permute-done((bf16[256,1536]{1,0:T(8,128)(2,1)S(1)}, bf16[256,1536]{1,0:T(8,128)(2,1)S(1)}, u32[]{:S(2)}, u32[]{:S(2)}) %collective-permute-start.18) | collective-permute-done | bytes 786464 | tf_op jit(solution)/shard_map/ppermute | solution.py:104
  279.0 16.7 %shard_map.371 = (bf16[2,1024,512]{2,1,0:T(8,128)(2,1)}, bf16[2,1024,1024]{2,1,0:T(8,128)(2,1)}) custom-call(s32[1]{0:T(128)} %bitcast.41.refs_0_, bf16[1024,1536]{1,0:T(8,128)(2,1)} %bitcast.110, f32[1024,5]{1,0:T(8,128)} %constant_dynamic-update-slice_fusion.refs_2_, bf16[2,1536,1536]{2,1,0:T(8,128)(2,1)} %all-gather.3.cloned.1.call-done.refs_3_, ...), custom_call_target="tpu_custom_call" | custom-call | flops 1 | bytes 1 | tf_op jit(solution)/shard_map/pallas_call | solution.py:473
  300.1 16.8 %shard_map.373 = bf16[2,1536,1536]{2,1,0:T(8,128)(2,1)} custom-call(bf16[1536,1024]{1,0:T(8,128)(2,1)} %shard_map.372.refs_0_, bf16[1536,1024]{1,0:T(8,128)(2,1)} %shard_map.369.refs_1_, bf16[2,1024,1024]{2,1,0:T(8,128)(2,1)} %get-tuple-element.158.refs_2_.refs_1_, bf16[2,1024,512]{2,1,0:T(8,128)(2,1)} %get-tuple-element.155.refs_3_.refs_1_, ...), custom_call_target="tpu_custom_call" | custom-call | flops 1 | bytes 1 | tf_op jit(solution)/shard_map/pallas_call | solution.py:554
  317.2 31.7 %all-gather.5.cloned.1.call-done.refs_3_.refs_4_ = bf16[3,1536,1536]{2,1,0:T(8,128)(2,1)} async-done(((bf16[3,192,1536]{2,1,0:T(8,128)(2,1)}), bf16[3,1536,1536]{2,1,0:T(8,128)(2,1)}) %all-gather.5.cloned.1.call-update) | async-done | bytes 14155792 | tf_op jit(solution)/shard_map/all_gather | solution.py:919
  348.9 21.6 %shard_map.374 = (bf16[3,1024,512]{2,1,0:T(8,128)(2,1)}, bf16[3,1024,1024]{2,1,0:T(8,128)(2,1)}) custom-call(s32[1]{0:T(128)} %bitcast.41.refs_0_, bf16[1024,1536]{1,0:T(8,128)(2,1)} %bitcast.111, f32[1024,5]{1,0:T(8,128)} %constant_dynamic-update-slice_fusion.refs_2_, bf16[3,1536,1536]{2,1,0:T(8,128)(2,1)} %all-gather.5.cloned.1.call-done.refs_3_.refs_4_, ...), custom_call_target="tpu_custom_call" | custom-call | flops 1 | bytes 1 | tf_op jit(solution)/shard_map/pallas_call | solution.py:473
  370.4 24.1 %shard_map.375 = (bf16[256,1536]{1,0:T(8,128)(2,1)}, bf16[256,1536]{1,0:T(8,128)(2,1)}, bf16[256,1536]{1,0:T(8,128)(2,1)}, bf16[256,1536]{1,0:T(8,128)(2,1)}) custom-call(s32[1]{0:T(128)} %bitcast.41.refs_0_, bf16[2,1024,1024]{2,1,0:T(8,128)(2,1)} %get-tuple-element.158.refs_2_.refs_1_, bf16[3,1024,1024]{2,1,0:T(8,128)(2,1)} %get-tuple-element.161.refs_2_, ...), custom_call_target="tpu_custom_call" | custom-call | flops 1 | bytes 1 | tf_op jit(solution)/shard_map/pallas_call | solution.py:615
  398.6 23.6 %shard_map.376 = bf16[3,1536,1536]{2,1,0:T(8,128)(2,1)} custom-call(bf16[1536,1024]{1,0:T(8,128)(2,1)} %shard_map.372.refs_0_, bf16[1536,1024]{1,0:T(8,128)(2,1)} %shard_map.369.refs_1_, bf16[3,1024,1024]{2,1,0:T(8,128)(2,1)} %get-tuple-element.161.refs_2_, bf16[3,1024,512]{2,1,0:T(8,128)(2,1)} %get-tuple-element.160.refs_3_.refs_2_, ...), custom_call_target="tpu_custom_call" | custom-call | flops 1 | bytes 1 | tf_op jit(solution)/shard_map/pallas_call | solution.py:554
  422.1 14.6 %shard_map.377 = (bf16[256,1536]{1,0:T(8,128)(2,1)}, bf16[256,1536]{1,0:T(8,128)(2,1)}, bf16[256,1536]{1,0:T(8,128)(2,1)}, bf16[256,1536]{1,0:T(8,128)(2,1)}) custom-call(s32[1]{0:T(128)} %bitcast.41.refs_0_, bf16[2,1024,512]{2,1,0:T(8,128)(2,1)} %get-tuple-element.155.refs_3_.refs_1_, bf16[3,1024,512]{2,1,0:T(8,128)(2,1)} %get-tuple-element.160.refs_3_.refs_2_, ...), custom_call_target="tpu_custom_call" | custom-call | flops 1 | bytes 1 | tf_op jit(solution)/shard_map/pallas_call | solution.py:615
  438.8 8.3 %shard_map.378 = (f32[256,1536]{1,0:T(8,128)}, bf16[1536,256]{1,0:T(8,128)(2,1)}, bf16[256,1536]{1,0:T(8,128)(2,1)}, bf16[1536,128]{1,0:T(8,128)(2,1)}) custom-call(f32[256,1]{1,0:T(8,128)} %copy.140.refs_0_, f32[1,1536]{1,0:T(1,128)} %reshape.434.refs_1_, f32[256,1536]{1,0:T(8,128)} %copy-done.4, bf16[256,1536]{1,0:T(8,128)(2,1)} %bitcast.129, ...), custom_call_target="tpu_custom_call" | custom-call | flops 1 | bytes 1 | tf_op jit(solution)/shard_map/pallas_call | solution.py:650
  452.7 20.3 %shard_map.379 = (bf16[256,1536]{1,0:T(8,128)(2,1)}, bf16[4,256,1024]{2,1,0:T(8,128)(2,1)}) custom-call(s32[1]{0:T(128)} %bitcast.42.refs_0_, bf16[256,1536]{1,0:T(8,128)(2,1)} %get-tuple-element.135.refs_0_.refs_1_, bf16[256,1536]{1,0:T(8,128)(2,1)} %get-tuple-element.173.refs_2_, f32[256,1536]{1,0:T(8,128)} %get-tuple-element.174.refs_3_, ...), custom_call_target="tpu_custom_call" | custom-call | flops 1 | bytes 1 | tf_op jit(solution)/shard_map/pallas_call | solution.py:413
  473.0 14.8 %collective-permute-done.21 = bf16[256,1536]{1,0:T(8,128)(2,1)S(1)} collective-permute-done((bf16[256,1536]{1,0:T(8,128)(2,1)}, bf16[256,1536]{1,0:T(8,128)(2,1)S(1)}, u32[]{:S(2)}, u32[]{:S(2)}) %collective-permute-start.21) | collective-permute-done | bytes 786464 | tf_op jit(solution)/shard_map/ppermute | solution.py:104
  490.3 5.5 shard_map.380
  500.5 5.5 shard_map.381.refs_0_
  506.0 7.6 %shard_map.382 = (bf16[192,3200]{1,0:T(8,128)(2,1)}, bf16[192,3200]{1,0:T(8,128)(2,1)}, bf16[192,3200]{1,0:T(8,128)(2,1)}, bf16[192,3200]{1,0:T(8,128)(2,1)}) custom-call(bf16[768,3200]{1,0:T(8,128)(2,1)} %shard_map.381.refs_0_, bf16[768,3200]{1,0:T(8,128)(2,1)} %collective-permute-done.26.refs_1_, ...), custom_call_target="tpu_custom_call" | custom-call | flops 1 | bytes 1 | tf_op jit(solution)/shard_map/pallas_call | solution.py:172
  516.3 26.0 %collective-permute-done.27.refs_1_ = bf16[192,3200]{1,0:T(8,128)(2,1)S(1)} collective-permute-done((bf16[192,3200]{1,0:T(8,128)(2,1)}, bf16[192,3200]{1,0:T(8,128)(2,1)S(1)}, u32[]{:S(2)}, u32[]{:S(2)}) %collective-permute-start.27) | collective-permute-done | bytes 1228832 | tf_op jit(solution)/shard_map/ppermute | solution.py:104
  543.1 26.7 %collective-permute-done.29.refs_3_ = bf16[192,3200]{1,0:T(8,128)(2,1)} collective-permute-done((bf16[192,3200]{1,0:T(8,128)(2,1)}, bf16[192,3200]{1,0:T(8,128)(2,1)}, u32[]{:S(2)}, u32[]{:S(2)}) %collective-permute-start.29) | collective-permute-done | bytes 1228832 | tf_op jit(solution)/shard_map/ppermute | solution.py:104
  605.4 8.4 %shard_map.386 = bf16[256,1536]{1,0:T(8,128)(2,1)} custom-call(s32[32]{0:T(128)} %copy-done.42, bf16[256,1536]{1,0:T(8,128)(2,1)} %get-tuple-element.177.refs_4_.refs_1_, bf16[256,1024]{1,0:T(8,128)(2,1)} %get-tuple-element.197.refs_2_, f32[256,1]{1,0:T(8,128)} %copy.137.refs_1_.refs_7_.refs_3_, bf16[256,1536]{1,0:T(8,128)(2,1)} %bitcast.126, ...), custom_call_target="tpu_custom_call" | custom-call | flops 1 | bytes 1 | tf_op jit(solution)/shard_map/pallas_call | solution.py:768
  624.4 6.7 shard_map.388
  631.1 43.5 %reduce-scatter.5.cloned.1.call-done.refs_0_ = bf16[3,192,1536]{2,1,0:T(8,128)(2,1)} async-done(((bf16[3,1536,1536]{2,1,0:T(8,128)(2,1)}), bf16[3,192,1536]{2,1,0:T(8,128)(2,1)}) %reduce-scatter.5.cloned.1.call-update) | async-done | bytes 1769488 | tf_op jit(solution)/shard_map/reduce_scatter | solution.py:1011
  674.6 11.0 %shard_map.389 = (f32[5,192,1024]{2,1,0:T(8,128)}, f32[5,192,1024]{2,1,0:T(8,128)}, f32[5,192,1024]{2,1,0:T(8,128)}, f32[5,192,512]{2,1,0:T(8,128)}, f32[5,192,512]{2,1,0:T(8,128)}, /*index=5*/f32[5,192,512]{2,1,0:T(8,128)}) custom-call(bf16[3,192,1536]{2,1,0:T(8,128)(2,1)} %reduce-scatter.5., ...), custom_call_target="tpu_custom_call", output_to_operand_aliasing={{0}: (7, {}), {1}: (8, {}), {2}: (9, {}), {3}: (10, {}), {4... | custom-call | flops 1 | bytes 1 | tf_op jit(solution)/shard_map/pallas_call | solution.py:795
  686.6 9.0 %shard_map.390 = (f32[48,2560]{1,0:T(8,128)}, f32[48,2560]{1,0:T(8,128)}, f32[48,2560]{1,0:T(8,128)}, f32[48,1536]{1,0:T(8,128)}, f32[48,1536]{1,0:T(8,128)}, /*...) custom-call(f32[384,384]{1,0:T(8,128)} %constant.88.refs_0_, ...), custom_call_target="tpu_custom_call" | custom-call | flops 1 | bytes 1 | tf_op jit(solution)/shard_map/pallas_call | solution.py:845
  (292 shorter events, 153.5 us)
Async XLA Ops:
  7.2 271.8 %all-gather.3.cloned.1.call-start = ((), (), s32[]{:S(2)}) async-start(), calls=%async_computation.5 | async-start | bytes 10616832 | tf_op jit(solution)/shard_map/all_gather | solution.py:919
  12.9 28.1 %collective-permute-start.2 = (bf16[48,4224]{1,0:T(8,128)(2,1)}, bf16[48,4224]{1,0:T(8,128)(2,1)S(1)}, u32[]{:S(2)}, u32[]{:S(2)}) collective-permute-start(bf16[48,4224]{1,0:T(8,128)(2,1)} %pad_maximum_fusion.4), channel_id=1, source_target_pairs={{0,6},{2,4},{4,2},{6,0},{1,7},{3,5},{5,3},{7,1},{8,14},{10,12},{12... | collective-permute-start | bytes 1216520 | tf_op jit(solution)/shard_map/ppermute | solution.py:104
  14.2 34.4 %collective-permute-start.1 = (bf16[48,4224]{1,0:T(8,128)(2,1)}, bf16[48,4224]{1,0:T(8,128)(2,1)}, u32[]{:S(2)}, u32[]{:S(2)}) collective-permute-start(bf16[48,4224]{1,0:T(8,128)(2,1)} %pad_maximum_fusion.4), channel_id=1, source_target_pairs={{0,4},{2,6},{4,0},{6,2},{1,5},{3,7},{5,1},{7,3},{8,12},{10,14},{12... | collective-permute-start | bytes 1216520 | tf_op jit(solution)/shard_map/ppermute | solution.py:104
  15.3 33.4 %collective-permute-start = (bf16[48,4224]{1,0:T(8,128)(2,1)}, bf16[48,4224]{1,0:T(8,128)(2,1)}, u32[]{:S(2)}, u32[]{:S(2)}) collective-permute-start(bf16[48,4224]{1,0:T(8,128)(2,1)} %pad_maximum_fusion.4), channel_id=1, source_target_pairs={{0,2},{2,0},{4,6},{6,4},{1,3},{3,1},{5,7},{7,5},{8,10},{10,8},{12,... | collective-permute-start | bytes 1216520 | tf_op jit(solution)/shard_map/ppermute | solution.py:104
  54.5 43.6 %collective-permute-start.4 = (bf16[192,2560]{1,0:T(8,128)(2,1)S(1)}, bf16[192,2560]{1,0:T(8,128)(2,1)}, u32[]{:S(2)}, u32[]{:S(2)}) collective-permute-start(bf16[192,2560]{1,0:T(8,128)(2,1)S(1)} %slice.53.refs_4_.refs_6_), channel_id=1, source_target_pairs={{0,16},{8,24},{16,0},{24,8},{1,17},{9,25},{17,1},{25,9},{2,18},{10... | collective-permute-start | bytes 2949128 | tf_op jit(solution)/shard_map/ppermute | solution.py:104
  54.7 43.3 %collective-permute-start.3 = (bf16[192,2560]{1,0:T(8,128)(2,1)S(1)}, bf16[192,2560]{1,0:T(8,128)(2,1)}, u32[]{:S(2)}, u32[]{:S(2)}) collective-permute-start(bf16[192,2560]{1,0:T(8,128)(2,1)S(1)} %slice.53.refs_4_.refs_6_), channel_id=1, source_target_pairs={{0,8},{8,0},{16,24},{24,16},{1,9},{9,1},{17,25},{25,17},{2,10},{10... | collective-permute-start | bytes 2949128 | tf_op jit(solution)/shard_map/ppermute | solution.py:104
  64.4 38.3 %collective-permute-start.6 = (bf16[192,2560]{1,0:T(8,128)(2,1)S(1)}, bf16[192,2560]{1,0:T(8,128)(2,1)S(1)}, u32[]{:S(2)}, u32[]{:S(2)}) collective-permute-start(bf16[192,2560]{1,0:T(8,128)(2,1)S(1)} %slice.53.refs_4_.refs_6_), channel_id=1, source_target_pairs={{0,1},{1,0},{2,3},{3,2},{4,5},{5,4},{6,7},{7,6},{8,9},{9,8},{10,11... | collective-permute-start | bytes 2949128 | tf_op jit(solution)/shard_map/ppermute | solution.py:104
  147.8 56.2 %collective-permute-start.13 = (bf16[4,192,1664]{2,1,0:T(8,128)(2,1)}, bf16[4,192,1664]{2,1,0:T(8,128)(2,1)}, u32[]{:S(2)}, u32[]{:S(2)}) collective-permute-start(bf16[4,192,1664]{2,1,0:T(8,128)(2,1)} %all_to_all.15), channel_id=1, source_target_pairs={{0,1},{1,0},{2,3},{3,2},{4,5},{5,4},{6,7},{7,6},{8,9},{9,8},{10,11... | collective-permute-start | bytes 7667720 | tf_op jit(solution)/shard_map/ppermute | solution.py:104
  151.1 63.8 %all-to-all-start.1 = ((bf16[4,256,1536]{2,1,0:T(8,128)(2,1)}), bf16[4,256,1536]{2,1,0:T(8,128)(2,1)S(1)}, u32[]{:S(2)}, u32[]{:S(2)}) async-start(bf16[4,256,1536]{2,1,0:T(8,128)(2,1)} %broadcast_in_dim.36), calls=%async_computation.1 | async-start | bytes 6291456 | tf_op jit(solution)/shard_map/all_to_all | solution.py:125
  154.9 194.0 %all-gather.5.cloned.1.call-start = ((), (), s32[]{:S(2)}) async-start(), calls=%async_computation.6 | async-start | bytes 15925248 | tf_op jit(solution)/shard_map/all_gather | solution.py:919
  155.2 38.9 %collective-permute-start.14 = (f32[256,5]{1,0:T(8,128)}, f32[256,5]{1,0:T(8,128)}, u32[]{:S(2)}, u32[]{:S(2)}) collective-permute-start(f32[256,5]{1,0:T(8,128)} %bitcast.157), channel_id=1, source_target_pairs={{0,8},{8,0},{16,24},{24,16},{1,9},{9,1},{17,25},{25,17},{2,10},{10... | collective-permute-start | bytes 15368 | tf_op jit(solution)/shard_map/ppermute | solution.py:104
  156.6 40.4 %collective-permute-start.15 = (f32[256,5]{1,0:T(8,128)S(1)}, f32[256,5]{1,0:T(8,128)}, u32[]{:S(2)}, u32[]{:S(2)}) collective-permute-start(f32[256,5]{1,0:T(8,128)S(1)} %bitcast.156), channel_id=1, source_target_pairs={{0,16},{8,24},{16,0},{24,8},{1,17},{9,25},{17,1},{25,9},{2,18},{10... | collective-permute-start | bytes 15368 | tf_op jit(solution)/shard_map/ppermute | solution.py:104
  157.8 40.0 %collective-permute-start.16 = (f32[256,5]{1,0:T(8,128)S(1)}, f32[256,5]{1,0:T(8,128)}, u32[]{:S(2)}, u32[]{:S(2)}) collective-permute-start(f32[256,5]{1,0:T(8,128)S(1)} %bitcast.155), channel_id=1, source_target_pairs={{0,24},{8,16},{16,8},{24,0},{1,25},{9,17},{17,9},{25,1},{2,26},{10... | collective-permute-start | bytes 15368 | tf_op jit(solution)/shard_map/ppermute | solution.py:104
  157.9 63.2 %collective-permute-start.12 = (bf16[256,1024]{1,0:T(8,128)(2,1)}, bf16[256,1024]{1,0:T(8,128)(2,1)}, u32[]{:S(2)}, u32[]{:S(2)}) collective-permute-start(bf16[256,1024]{1,0:T(8,128)(2,1)} %get-tuple-element.149.refs_3_.refs_10_), channel_id=1, source_target_pairs={{0,6},{2,4},{4,2},{6,0},{1,7},{3,5},{5,3},{7,1},{8,14},{10,12},{12... | collective-permute-start | bytes 1572872 | tf_op jit(solution)/shard_map/ppermute | solution.py:104
  221.1 228.9 %reduce-scatter.3.cloned.1.call-start = ((), (), s32[]{:S(2)}) async-start(), calls=%async_computation.7 | async-start | bytes 10616832 | tf_op jit(solution)/shard_map/reduce_scatter | solution.py:1011
  242.1 35.9 %collective-permute-start.18 = (bf16[256,1536]{1,0:T(8,128)(2,1)S(1)}, bf16[256,1536]{1,0:T(8,128)(2,1)S(1)}, u32[]{:S(2)}, u32[]{:S(2)}) collective-permute-start(bf16[256,1536]{1,0:T(8,128)(2,1)S(1)} %multiply_convert_fusion.refs_4_.refs_1_), channel_id=1, source_target_pairs={{0,16},{8,24},{16,0},{24,8},{1,17},{9,25},{17,1},{25,9},{2,18},{10... | collective-permute-start | bytes 2359304 | tf_op jit(solution)/shard_map/ppermute | solution.py:104
  243.1 35.8 %collective-permute-start.17 = (bf16[256,1536]{1,0:T(8,128)(2,1)S(1)}, bf16[256,1536]{1,0:T(8,128)(2,1)}, u32[]{:S(2)}, u32[]{:S(2)}) collective-permute-start(bf16[256,1536]{1,0:T(8,128)(2,1)S(1)} %multiply_convert_fusion.refs_4_.refs_1_), channel_id=1, source_target_pairs={{0,8},{8,0},{16,24},{24,16},{1,9},{9,1},{17,25},{25,17},{2,10},{10... | collective-permute-start | bytes 2359304 | tf_op jit(solution)/shard_map/ppermute | solution.py:104
  316.9 357.6 %reduce-scatter.5.cloned.1.call-start = ((), (), s32[]{:S(2)}) async-start(), calls=%async_computation.8 | async-start | bytes 15925248 | tf_op jit(solution)/shard_map/reduce_scatter | solution.py:1011
  394.5 42.2 %collective-permute-start.23 = (bf16[256,1536]{1,0:T(8,128)(2,1)}, bf16[256,1536]{1,0:T(8,128)(2,1)S(1)}, u32[]{:S(2)}, u32[]{:S(2)}) collective-permute-start(bf16[256,1536]{1,0:T(8,128)(2,1)} %get-tuple-element.163), channel_id=1, source_target_pairs={{0,8},{8,0},{16,24},{24,16},{1,9},{9,1},{17,25},{25,17},{2,10},{10... | collective-permute-start | bytes 2359304 | tf_op jit(solution)/shard_map/ppermute | solution.py:104
  395.9 40.8 %collective-permute-start.24 = (bf16[256,1536]{1,0:T(8,128)(2,1)}, bf16[256,1536]{1,0:T(8,128)(2,1)S(1)}, u32[]{:S(2)}, u32[]{:S(2)}) collective-permute-start(bf16[256,1536]{1,0:T(8,128)(2,1)} %get-tuple-element.164), channel_id=1, source_target_pairs={{0,16},{8,24},{16,0},{24,8},{1,17},{9,25},{17,1},{25,9},{2,18},{10... | collective-permute-start | bytes 2359304 | tf_op jit(solution)/shard_map/ppermute | solution.py:104
  397.1 39.6 %collective-permute-start.25 = (bf16[256,1536]{1,0:T(8,128)(2,1)}, bf16[256,1536]{1,0:T(8,128)(2,1)S(1)}, u32[]{:S(2)}, u32[]{:S(2)}) collective-permute-start(bf16[256,1536]{1,0:T(8,128)(2,1)} %get-tuple-element.165), channel_id=1, source_target_pairs={{0,24},{8,16},{16,8},{24,0},{1,25},{9,17},{17,9},{25,1},{2,26},{10... | collective-permute-start | bytes 2359304 | tf_op jit(solution)/shard_map/ppermute | solution.py:104
  451.2 36.6 %collective-permute-start.21 = (bf16[256,1536]{1,0:T(8,128)(2,1)}, bf16[256,1536]{1,0:T(8,128)(2,1)S(1)}, u32[]{:S(2)}, u32[]{:S(2)}) collective-permute-start(bf16[256,1536]{1,0:T(8,128)(2,1)} %get-tuple-element.170), channel_id=1, source_target_pairs={{0,16},{8,24},{16,0},{24,8},{1,17},{9,25},{17,1},{25,9},{2,18},{10... | collective-permute-start | bytes 2359304 | tf_op jit(solution)/shard_map/ppermute | solution.py:104
  452.4 35.4 %collective-permute-start.22 = (bf16[256,1536]{1,0:T(8,128)(2,1)}, bf16[256,1536]{1,0:T(8,128)(2,1)}, u32[]{:S(2)}, u32[]{:S(2)}) collective-permute-start(bf16[256,1536]{1,0:T(8,128)(2,1)} %get-tuple-element.171), channel_id=1, source_target_pairs={{0,24},{8,16},{16,8},{24,0},{1,25},{9,17},{17,9},{25,1},{2,26},{10... | collective-permute-start | bytes 2359304 | tf_op jit(solution)/shard_map/ppermute | solution.py:104
  496.4 82.7 %all-to-all-start.2 = ((bf16[4,256,1024]{2,1,0:T(8,128)(2,1)}), bf16[4,256,1024]{2,1,0:T(8,128)(2,1)S(1)}, u32[]{:S(2)}, u32[]{:S(2)}) async-start(bf16[4,256,1024]{2,1,0:T(8,128)(2,1)} %get-tuple-element.182), calls=%async_computation.3 | async-start | bytes 4194304 | tf_op jit(solution)/shard_map/all_to_all | solution.py:125
  513.6 28.6 %collective-permute-start.27 = (bf16[192,3200]{1,0:T(8,128)(2,1)}, bf16[192,3200]{1,0:T(8,128)(2,1)S(1)}, u32[]{:S(2)}, u32[]{:S(2)}) collective-permute-start(bf16[192,3200]{1,0:T(8,128)(2,1)} %get-tuple-element.189), channel_id=1, source_target_pairs={{0,8},{8,0},{16,24},{24,16},{1,9},{9,1},{17,25},{25,17},{2,10},{10... | collective-permute-start | bytes 3686408 | tf_op jit(solution)/shard_map/ppermute | solution.py:104
  514.7 28.3 %collective-permute-start.28 = (bf16[192,3200]{1,0:T(8,128)(2,1)}, bf16[192,3200]{1,0:T(8,128)(2,1)}, u32[]{:S(2)}, u32[]{:S(2)}) collective-permute-start(bf16[192,3200]{1,0:T(8,128)(2,1)} %get-tuple-element.190), channel_id=1, source_target_pairs={{0,16},{8,24},{16,0},{24,8},{1,17},{9,25},{17,1},{25,9},{2,18},{10... | collective-permute-start | bytes 3686408 | tf_op jit(solution)/shard_map/ppermute | solution.py:104
  515.1 54.6 %collective-permute-start.29 = (bf16[192,3200]{1,0:T(8,128)(2,1)}, bf16[192,3200]{1,0:T(8,128)(2,1)}, u32[]{:S(2)}, u32[]{:S(2)}) collective-permute-start(bf16[192,3200]{1,0:T(8,128)(2,1)} %get-tuple-element.191), channel_id=1, source_target_pairs={{0,24},{8,16},{16,8},{24,0},{1,25},{9,17},{17,9},{25,1},{2,26},{10... | collective-permute-start | bytes 3686408 | tf_op jit(solution)/shard_map/ppermute | solution.py:104
  599.5 86.2 %collective-permute-start.32 = (bf16[48,3200]{1,0:T(8,128)(2,1)S(1)}, bf16[48,3200]{1,0:T(8,128)(2,1)S(1)}, u32[]{:S(2)}, u32[]{:S(2)}) collective-permute-start(bf16[48,3200]{1,0:T(8,128)(2,1)S(1)} %copy-done.55), channel_id=1, source_target_pairs={{0,4},{2,6},{4,0},{6,2},{1,5},{3,7},{5,1},{7,3},{8,12},{10,14},{12... | collective-permute-start | bytes 921608 | tf_op jit(solution)/shard_map/ppermute | solution.py:104
  604.3 81.3 %collective-permute-start.33 = (bf16[48,3200]{1,0:T(8,128)(2,1)S(1)}, bf16[48,3200]{1,0:T(8,128)(2,1)S(1)}, u32[]{:S(2)}, u32[]{:S(2)}) collective-permute-start(bf16[48,3200]{1,0:T(8,128)(2,1)S(1)} %copy-done.54), channel_id=1, source_target_pairs={{0,6},{2,4},{4,2},{6,0},{1,7},{3,5},{5,3},{7,1},{8,14},{10,12},{12... | collective-permute-start | bytes 921608 | tf_op jit(solution)/shard_map/ppermute | solution.py:104
  617.5 68.1 %collective-permute-start.37 = (bf16[48,1024]{1,0:T(8,128)(2,1)}, bf16[48,1024]{1,0:T(8,128)(2,1)S(1)}, u32[]{:S(2)}, u32[]{:S(2)}) collective-permute-start(bf16[48,1024]{1,0:T(8,128)(2,1)} %get-tuple-element.210), channel_id=1, source_target_pairs={{0,2},{2,0},{4,6},{6,4},{1,3},{3,1},{5,7},{7,5},{8,10},{10,8},{12,... | collective-permute-start | bytes 294920 | tf_op jit(solution)/shard_map/ppermute | solution.py:104
  621.1 64.6 %collective-permute-start.38 = (bf16[48,1024]{1,0:T(8,128)(2,1)}, bf16[48,1024]{1,0:T(8,128)(2,1)S(1)}, u32[]{:S(2)}, u32[]{:S(2)}) collective-permute-start(bf16[48,1024]{1,0:T(8,128)(2,1)} %get-tuple-element.211), channel_id=1, source_target_pairs={{0,4},{2,6},{4,0},{6,2},{1,5},{3,7},{5,1},{7,3},{8,12},{10,14},{12... | collective-permute-start | bytes 294920 | tf_op jit(solution)/shard_map/ppermute | solution.py:104
  621.7 64.0 %collective-permute-start.39 = (bf16[48,1024]{1,0:T(8,128)(2,1)}, bf16[48,1024]{1,0:T(8,128)(2,1)S(1)}, u32[]{:S(2)}, u32[]{:S(2)}) collective-permute-start(bf16[48,1024]{1,0:T(8,128)(2,1)} %get-tuple-element.212), channel_id=1, source_target_pairs={{0,6},{2,4},{4,2},{6,0},{1,7},{3,5},{5,3},{7,1},{8,14},{10,12},{12... | collective-permute-start | bytes 294920 | tf_op jit(solution)/shard_map/ppermute | solution.py:104
  (72 other events, 970.0 us)
Sparse Core Ops, SparseCore 0:
  50.2 91.2 all-gather.2
  221.2 127.5 all-gather.4
  351.2 98.7 reduce-scatter.2
  452.1 222.3 reduce-scatter.4
